TPU v7x, 128 devices: a whole 4x4x4 slice. The times are simulated.
128 devices in a mesh: row: 8 (over y_hi, x), col: 8 (over z, y_lo), layer: 2 (over core).
Axes of the slice: x: 4, y: 4 (y_hi: 2, y_lo: 2; y = y_hi * 2 + y_lo), z: 4, core: 2. Of those that a mesh axis runs over, the one named last changes fastest.
Arguments:
- similarity: bfloat16 [12288, 12288], P('row', ('col', 'layer')), may hold values from 0.049804688 to 1
- block_mask: int32 [96, 96], P('row', ('col', 'layer')), may hold values from 0 to 1, as said below
Outputs:
- normalized: float32 [12288, 12288], P('row', ('col', 'layer'))
Inputs may be any that keep to these rules, and one draw needn't show every extreme that they name: Entries are 0 or 1; every diagonal block is 1; each device's share of block_mask holds at most 18 ones, and some device's share holds exactly 18.
All inputs are finite; a program needn't handle non-finite values.
Results may differ from a plain program's by a relative error of at most 0.0003.
Values may be sent and summed in bfloat16 or wider, within the bound.
A program may use at most 256 MiB of HBM per device.

v0:
```python
import jax
import jax.numpy as jnp
from jax import lax
from jax.sharding import PartitionSpec as P

BLK = 128


def body(similarity, block_mask):
    expanded = jnp.repeat(jnp.repeat(block_mask, BLK, 0), BLK, 1).astype(similarity.dtype)
    masked = similarity * expanded
    tile_rows, tile_cols = masked.shape
    full_tile = lax.all_gather(masked, "layer", axis=1, tiled=True)
    half_rows = tile_rows // lax.axis_size("layer")
    own_half = lax.dynamic_slice_in_dim(
        full_tile, lax.axis_index("layer") * half_rows, half_rows, 0
    )
    inner_panel = lax.all_gather(own_half, "row", axis=0, tiled=True)
    partial_value = jnp.dot(
        lax.all_gather(masked, "col", axis=1, tiled=True),
        inner_panel,
        preferred_element_type=jnp.float32,
    )
    product = lax.psum_scatter(partial_value, "layer", scatter_dimension=1, tiled=True)
    inflated = product * product
    totals = lax.psum(jnp.sum(inflated, axis=0), "row")
    scaling = tile_rows * lax.axis_size("row")
    return scaling * inflated / totals


def solution(mesh):
    return jax.shard_map(
        body,
        mesh=mesh,
        in_specs=(P("row", ("col", "layer")), P("row", ("col", "layer"))),
        out_specs=P("row", ("col", "layer")),
        check_vma=False,
    )
```

profile of v0, /device:TPU:0, one launch (start us, length us, event | category | flops | bytes accessed | tf_op | source)
XLA Modules:
  0.0 700.9 jit_solution(7120083691532146629)
XLA Ops:
  6.5 0.0 all-gather.6.cloned.1.call-start
  6.5 0.7 convert_element_type.11
  7.2 0.1 broadcast_bitcast_fusion
  7.3 2.8 copy.4
  10.2 1.6 bitcast_multiply_fusion
  11.7 0.0 all-gather.6.cloned.1.call-update
  11.8 0.0 all-gather.4.cloned.1.call-start
  11.8 0.7 all-gather.4.cloned.1.call-update
  12.5 0.0 all-gather.8.cloned.1.call-start
  12.6 18.9 %all-gather.6.cloned.1.call-done = bf16[1536,1536]{0,1:T(8,128)(2,1)} async-done(((bf16[1536,768]{0,1:T(8,128)(2,1)}), bf16[1536,1536]{0,1:T(8,128)(2,1)}) %all-gather.6.cloned.1.call-update) | async-done | bytes 4718608 | tf_op jit(solution)/shard_map/all_gather | solution.py:13
  31.5 3.2 constant_dynamic-slice_fusion
  34.7 0.0 all-gather.8.cloned.1.call-update
  34.7 0.0 reduce-scatter.2.cloned.1.call-start
  34.8 364.7 %all-gather.4.cloned.1.call-done = bf16[1536,6144]{0,1:T(8,128)(2,1)} async-done(((bf16[1536,768]{0,1:T(8,128)(2,1)}), bf16[1536,6144]{0,1:T(8,128)(2,1)}) %all-gather.4.cloned.1.call-update) | async-done | bytes 18874384 | tf_op jit(solution)/shard_map/all_gather | solution.py:20
  399.5 206.4 %all-gather.8.cloned.1.call-done = bf16[6144,1536]{0,1:T(8,128)(2,1)} async-done(((bf16[768,1536]{0,1:T(8,128)(2,1)}), bf16[6144,1536]{0,1:T(8,128)(2,1)}) %all-gather.8.cloned.1.call-update) | async-done | bytes 18874384 | tf_op jit(solution)/shard_map/all_gather | solution.py:18
  605.9 37.8 %fusion = f32[1536,1536]{1,0:T(8,128)} fusion(bf16[1536,6144]{0,1:T(8,128)(2,1)} %all-gather.4.cloned.1.call-done, bf16[6144,1536]{0,1:T(8,128)(2,1)} %all-gather.8.cloned.1.call-done), kind=kOutput, calls=%fused_computation.6 | convolution fusion | flops 28991029248 | bytes 47185920 | tf_op jit(solution)/shard_map/dot_general | solution.py:19
  643.7 0.0 reduce-scatter.2.cloned.1.call-update
  643.7 18.7 %reduce-scatter.2.cloned.1.call-done = f32[1536,768]{1,0:T(8,128)} async-done(((f32[1536,1536]{1,0:T(8,128)}), f32[1536,768]{1,0:T(8,128)}) %reduce-scatter.2.cloned.1.call-update) | async-done | bytes 4718608 | tf_op jit(solution)/shard_map/reduce_scatter | solution.py:24
  662.4 2.7 multiply_reduce_fusion
  665.2 24.2 %psum.7 = f32[768]{0:T(1024)S(1)} all-reduce(f32[768]{0:T(1024)S(1)} %multiply_reduce_fusion), channel_id=1, replica_groups=mesh['row'=8,'col'=8,'layer'=2] {'row'}, use_global_device_ids=true, to_apply=%region_2.0 | all-reduce | flops 768 | bytes 6144 | tf_op jit(solution)/shard_map/psum | solution.py:26
  689.3 5.0 multiply_divide_fusion
  (1 shorter events, 0.0 us)
Async XLA Ops:
  6.5 25.0 %all-gather.6.cloned.1.call-start = ((), (), s32[]{:S(2)}) async-start(), calls=%async_computation.2 | async-start | bytes 7077888 | tf_op jit(solution)/shard_map/all_gather | solution.py:13
  11.8 387.7 %all-gather.4.cloned.1.call-start = ((), (), s32[]{:S(2)}) async-start(), calls=%async_computation.1 | async-start | bytes 21233664 | tf_op jit(solution)/shard_map/all_gather | solution.py:20
  12.5 593.4 %all-gather.8.cloned.1.call-start = ((), (), s32[]{:S(2)}) async-start(), calls=%async_computation.3 | async-start | bytes 21233664 | tf_op jit(solution)/shard_map/all_gather | solution.py:18
  34.7 627.7 %reduce-scatter.2.cloned.1.call-start = ((), (), s32[]{:S(2)}) async-start(), calls=%async_computation.4 | async-start | bytes 14155776 | tf_op jit(solution)/shard_map/reduce_scatter | solution.py:24
Sparse Core Ops, SparseCore 0:
  11.9 19.5 all-gather.5
  33.1 366.2 all-gather.3
  401.8 204.0 all-gather.7
  643.8 18.5 reduce-scatter.1
where the time goes:
time: 701 us
  waiting for transfers between devices  610 us (87%)
  matrix products  37.8 us (5%)
  blocking collectives  24.2 us (3%)
  between operations  13.1 us (2%)
  other arithmetic  10 us (1%)
    all_gather x1, waiting for transfers between devices, body(): lax.all_gather(masked, 'col', axis=1, tiled=True)  365 us
    all_gather x1, waiting for transfers between devices, body(): inner_panel = lax.all_gather(own_half, 'row', axis=0, tiled=True)  206 us
    dot_general x1, matrix products, body(): jnp.dot(lax.all_gather(masked, 'col', axis=1, tiled=True), inner_panel, p...  37.8 us
    psum x1, blocking collectives, body(): totals = lax.psum(jnp.sum(inflated, axis=0), 'row')  24.2 us
    all_gather x1, waiting for transfers between devices, body(): full_tile = lax.all_gather(masked, 'layer', axis=1, tiled=True)  18.9 us
    reduce_scatter x1, waiting for transfers between devices, body(): lax.psum_scatter(partial_value, 'layer', scatter_dimension=1, tiled=True)  18.7 us
  transfers between devices with their start and end apart: 4, of which 4 were waited for; matrix products, arithmetic and copies ran while one was open for 0% of the time, Pallas kernels for 0%

commit v1 on v0

v1 whole, which is shorter than its diff:
```python
import functools

import jax
import jax.numpy as jnp
from jax import lax
from jax.experimental import pallas as pl
from jax.experimental.pallas import tpu as pltpu
from jax.sharding import PartitionSpec as P

BLK = 128
MAXNZ = 18
HEAD = 16
HALF = MAXNZ // 2
SHARE = HEAD + MAXNZ * BLK
CUT = HEAD + HALF * BLK
MIB = 1 << 20
MESH = pl.DeviceIdType.MESH


def pack_kernel(mask_ref, x_ref, share_ref, sems):
    rows, cols = mask_ref.shape
    base = (2 * lax.axis_index("col") + lax.axis_index("layer")) * cols
    sub = lax.broadcasted_iota(jnp.int32, (HEAD, BLK), 0)
    lane = lax.broadcasted_iota(jnp.int32, (HEAD, BLK), 1)

    def one_row(i, carry):
        count, head = carry
        for j in range(cols):
            here = mask_ref[i, j]

            @pl.when(here > 0)
            def _():
                pltpu.make_async_copy(
                    x_ref.at[pl.ds(i * BLK, BLK), pl.ds(j * BLK, BLK)],
                    share_ref.at[pl.ds(pl.multiple_of(HEAD + count * BLK, HEAD), BLK)],
                    sems.at[count],
                ).start()

            cell = (sub == i) & (lane == base + j)
            place = (sub == rows) & (lane == count)
            head = jnp.where(cell & (here > 0), count + 1, head)
            head = jnp.where(place & (here > 0), i * cols + j + 1, head)
            count = count + here
        return count, head

    count, head = lax.fori_loop(
        0, rows, one_row, (jnp.int32(0), jnp.zeros((HEAD, BLK), jnp.int32))
    )
    share_ref[pl.ds(0, HEAD), :] = head.astype(jnp.float32).astype(share_ref.dtype)
    for s in range(MAXNZ):

        @pl.when(s < count)
        def _():
            pltpu.make_async_copy(
                x_ref.at[pl.ds(0, BLK), pl.ds(0, BLK)],
                share_ref.at[pl.ds(HEAD + s * BLK, BLK)],
                sems.at[s],
            ).wait()


def pack(block_mask, similarity):
    return pl.pallas_call(
        pack_kernel,
        out_shape=pltpu.VMEM((SHARE, BLK), similarity.dtype),
        in_specs=[
            pl.BlockSpec(memory_space=pltpu.SMEM),
            pl.BlockSpec(memory_space=pltpu.HBM),
        ],
        out_specs=pl.BlockSpec(memory_space=pltpu.VMEM),
        scratch_shapes=[pltpu.SemaphoreType.DMA((MAXNZ,))],
        compiler_params=pltpu.CompilerParams(vmem_limit_bytes=4 * MIB),
        name="pack",
    )(block_mask, similarity)


def gather_kernel(share_ref, rows_ref, cols_ref, send_sems, recv_sems, own_sems):
    row, col, layer = (lax.axis_index(a) for a in ("row", "col", "layer"))
    high, x = row // 4, row % 4
    z, low = col // 2, col % 2

    def along_z(step):
        return 2 * ((z + step) % 4) + low

    def along_x(step):
        return 4 * high + (x + step) % 4

    mate = 2 * z + 1 - low
    far = 4 * (1 - high) + x

    zp, zm = (row, along_z(1), layer), (row, along_z(3), layer)
    xp, xm = (along_x(1), col, layer), (along_x(3), col, layer)
    lo, hi = (row, mate, layer), (far, mate, layer)
    sib = (row, col, 1 - layer)

    barrier = pltpu.get_barrier_semaphore()
    for peer in (zp, zm, xp, xm, lo, hi, sib):
        pl.semaphore_signal(barrier, inc=1, device_id=peer, device_id_type=MESH)
    pl.semaphore_wait(barrier, 7)

    mine = 2 * col + layer
    keep = [
        pltpu.make_async_copy(share_ref, rows_ref.at[mine], own_sems.at[0]),
        pltpu.make_async_copy(share_ref, cols_ref.at[row], own_sems.at[1]),
    ]
    for copy in keep:
        copy.start()

    H1, H2, ALL = pl.ds(0, CUT), pl.ds(CUT, SHARE - CUT), pl.ds(0, SHARE)
    n = [0]
    started = []

    def send(src, dst, part, peer):
        k = n[0]
        n[0] += 1
        copy = pltpu.make_async_remote_copy(
            src_ref=src.at[part],
            dst_ref=dst.at[part],
            send_sem=send_sems.at[k],
            recv_sem=recv_sems.at[k],
            device_id=peer,
            device_id_type=MESH,
        )
        copy.start()
        started.append(copy)
        return k

    waited = set()

    def arrived(k, dst, part, peer):
        waited.add(k)
        pltpu.make_async_remote_copy(
            src_ref=dst.at[part],
            dst_ref=dst.at[part],
            send_sem=send_sems.at[k],
            recv_sem=recv_sems.at[k],
            device_id=peer,
            device_id_type=MESH,
        ).wait_recv()

    def r(c):
        return rows_ref.at[2 * c + layer]

    def rsib(c):
        return rows_ref.at[2 * c + 1 - layer]

    def c(q):
        return cols_ref.at[q]

    own_r, own_c = r(col), c(row)
    lo1 = send(share_ref, own_r, H1, lo)
    zp1 = send(share_ref, own_r, H1, zp)
    zm2 = send(share_ref, own_r, H2, zm)
    xp1 = send(share_ref, own_c, H1, xp)
    xm2 = send(share_ref, own_c, H2, xm)
    lo2 = send(share_ref, own_r, H2, lo)
    zp2 = send(share_ref, own_r, H2, zp)
    zm1 = send(share_ref, own_r, H1, zm)
    xp2 = send(share_ref, own_c, H2, xp)
    xm1 = send(share_ref, own_c, H1, xm)
    sb0 = send(share_ref, own_r, ALL, sib)

    y_r = r(mate)
    arrived(lo1, y_r, H1, lo)
    hi1 = send(y_r, c(row), H1, hi)
    yzp1 = send(y_r, y_r, H1, zp)
    arrived(lo2, y_r, H2, lo)
    hi2 = send(y_r, c(row), H2, hi)
    yzm2 = send(y_r, y_r, H2, zm)

    zm_r, zp_r, zz_r = r(along_z(3)), r(along_z(1)), r(along_z(2))
    xm_c, xp_c, xx_c = c(along_x(3)), c(along_x(1)), c(along_x(2))
    arrived(zp1, zm_r, H1, zm)
    fzp = send(zm_r, zm_r, H1, zp)
    arrived(zm2, zp_r, H2, zp)
    fzm = send(zp_r, zp_r, H2, zm)
    arrived(xp1, xm_c, H1, xm)
    fxp = send(xm_c, xm_c, H1, xp)
    arrived(xm2, xp_c, H2, xp)
    fxm = send(xp_c, xp_c, H2, xm)
    yzp2 = send(y_r, y_r, H2, zp)
    yzm1 = send(y_r, y_r, H1, zm)
    sb1 = send(y_r, y_r, ALL, sib)

    y_c = c(far)
    arrived(hi1, y_c, H1, hi)
    yxp1 = send(y_c, y_c, H1, xp)
    arrived(hi2, y_c, H2, hi)
    yxm2 = send(y_c, y_c, H2, xm)
    yxp2 = send(y_c, y_c, H2, xp)
    yxm1 = send(y_c, y_c, H1, xm)

    def other(q):
        return q + 1 - 2 * (q % 2)

    ym_r, yp_r, yy_r = (r(other(along_z(s))) for s in (3, 1, 2))
    arrived(yzp1, ym_r, H1, zm)
    gzp = send(ym_r, ym_r, H1, zp)
    arrived(yzm2, yp_r, H2, zp)
    gzm = send(yp_r, yp_r, H2, zm)

    def across(q):
        return c((q + 4) % 8)

    ym_c, yp_c, yy_c = (across(along_x(s)) for s in (3, 1, 2))
    arrived(yxp1, ym_c, H1, xm)
    gxp = send(ym_c, ym_c, H1, xp)
    arrived(yxm2, yp_c, H2, xp)
    gxm = send(yp_c, yp_c, H2, xm)

    arrived(zp2, zm_r, H2, zm)
    sb2 = send(zm_r, zm_r, ALL, sib)
    arrived(zm1, zp_r, H1, zp)
    sb3 = send(zp_r, zp_r, ALL, sib)
    arrived(fzp, zz_r, H1, zm)
    arrived(fzm, zz_r, H2, zp)
    sb4 = send(zz_r, zz_r, ALL, sib)
    arrived(yzp2, ym_r, H2, zm)
    sb5 = send(ym_r, ym_r, ALL, sib)
    arrived(yzm1, yp_r, H1, zp)
    sb6 = send(yp_r, yp_r, ALL, sib)
    arrived(gzp, yy_r, H1, zm)
    sb7 = send(yy_r, yy_r, H1, sib)
    arrived(gzm, yy_r, H2, zp)
    sb8 = send(yy_r, yy_r, H2, sib)

    arrived(xp2, xm_c, H2, xm)
    arrived(xm1, xp_c, H1, xp)
    arrived(fxp, xx_c, H1, xm)
    arrived(fxm, xx_c, H2, xp)
    arrived(yxp2, ym_c, H2, xm)
    arrived(yxm1, yp_c, H1, xp)
    arrived(gxp, yy_c, H1, xm)
    arrived(gxm, yy_c, H2, xp)

    arrived(sb0, rsib(col), ALL, sib)
    arrived(sb1, rsib(mate), ALL, sib)
    arrived(sb2, rsib(along_z(3)), ALL, sib)
    arrived(sb3, rsib(along_z(1)), ALL, sib)
    arrived(sb4, rsib(along_z(2)), ALL, sib)
    arrived(sb5, rsib(other(along_z(3))), ALL, sib)
    arrived(sb6, rsib(other(along_z(1))), ALL, sib)
    arrived(sb7, rsib(other(along_z(2))), H1, sib)
    arrived(sb8, rsib(other(along_z(2))), H2, sib)
    assert waited == set(range(n[0])) and n[0] == COPIES
    for copy in started:
        copy.wait_send()
    for copy in keep:
        copy.wait()


COPIES = 37


def gather(share):
    return pl.pallas_call(
        gather_kernel,
        out_shape=[
            pltpu.VMEM((16, SHARE, BLK), share.dtype),
            pltpu.VMEM((8, SHARE, BLK), share.dtype),
        ],
        in_specs=[pl.BlockSpec(memory_space=pltpu.VMEM)],
        out_specs=[pl.BlockSpec(memory_space=pltpu.VMEM)] * 2,
        scratch_shapes=[
            pltpu.SemaphoreType.DMA((COPIES,)),
            pltpu.SemaphoreType.DMA((COPIES,)),
            pltpu.SemaphoreType.DMA((2,)),
        ],
        compiler_params=pltpu.CompilerParams(
            collective_id=0, has_side_effects=True, vmem_limit_bytes=32 * MIB
        ),
        name="gather",
    )(share)


GROUP = 4


def product_kernel(
    r_ref, c_ref, out_ref, sums_ref, dense, head_v, head_s, place_v, place_s, lists, sems
):
    tiles, lanes = out_ref.shape[0] // BLK, out_ref.shape[1]
    wide = lanes // BLK
    head = r_ref[0, pl.ds(0, HEAD), :].astype(jnp.float32)
    for s in range(1, 16):
        head = head + r_ref[s, pl.ds(0, HEAD), :].astype(jnp.float32)
    head_v[...] = head.astype(jnp.int32)
    for q in range(8):
        top = c_ref[q, pl.ds(0, HEAD), :].astype(jnp.float32).astype(jnp.int32)
        place_v[pl.ds(q, 1), :] = top[tiles : tiles + 1, :]
    copies = [
        pltpu.make_async_copy(head_v, head_s, sems.at[0]),
        pltpu.make_async_copy(place_v, place_s, sems.at[1]),
    ]
    for copy in copies:
        copy.start()

    @pl.loop(0, dense.shape[0] // 256)
    def _(t):
        dense[pl.ds(pl.multiple_of(t * 256, 256), 256), :] = jnp.zeros((256, lanes), dense.dtype)

    for copy in copies:
        copy.wait()

    @pl.loop(0, 8)
    def _(q):
        @pl.loop(0, MAXNZ)
        def _(s):
            v = place_s[q, s] - 1

            @pl.when(v >= 0)
            def _():
                k = q * tiles + v // wide
                j = v % wide
                dense[
                    pl.ds(pl.multiple_of(k * BLK, BLK), BLK),
                    pl.ds(pl.multiple_of(j * BLK, BLK), BLK),
                ] = c_ref[q, pl.ds(pl.multiple_of(HEAD + s * BLK, HEAD), BLK), :]

    sums_ref[...] = jnp.zeros(sums_ref.shape, jnp.float32)

    @pl.loop(0, tiles)
    def _(i):
        def look(k, count):
            v = head_s[i, k]
            lists[0, count] = k
            lists[1, count] = v - 1
            return count + jnp.where(v > 0, 1, 0)

        count = lax.fori_loop(0, 8 * tiles, look, jnp.int32(0), unroll=8)
        for t in range(GROUP):
            lists[0, count + t] = 0
            lists[1, count + t] = 0
        here = pl.ds(pl.multiple_of(i * BLK, BLK), BLK)

        def part(g):
            left, right = [], []
            for t in range(GROUP):
                p = g * GROUP + t
                k, v = lists[0, p], lists[1, p]
                a = r_ref[k // wide, pl.ds(pl.multiple_of(HEAD + v * BLK, HEAD), BLK), :]
                left.append(jnp.where(p < count, a, jnp.zeros_like(a)))
                right.append(dense[pl.ds(pl.multiple_of(k * BLK, BLK), BLK), :])
            return jnp.dot(
                jnp.concatenate(left, 1),
                jnp.concatenate(right, 0),
                preferred_element_type=jnp.float32,
            )

        out_ref[here, :] = part(0)

        @pl.loop(1, (count + GROUP - 1) // GROUP)
        def _(g):
            out_ref[here, :] += part(g)

        value = out_ref[here, :]
        value = value * value
        out_ref[here, :] = value
        sums_ref[...] += jnp.sum(value.reshape(BLK // 8, 8, lanes), axis=0)


def product(rows, cols, out_rows, lanes):
    return pl.pallas_call(
        product_kernel,
        out_shape=[
            pltpu.VMEM((out_rows, lanes), jnp.float32),
            pltpu.VMEM((8, lanes), jnp.float32),
        ],
        in_specs=[pl.BlockSpec(memory_space=pltpu.VMEM)] * 2,
        out_specs=[pl.BlockSpec(memory_space=pltpu.VMEM)] * 2,
        scratch_shapes=[
            pltpu.VMEM((8 * out_rows, lanes), rows.dtype),
            pltpu.VMEM((HEAD, BLK), jnp.int32),
            pltpu.SMEM((HEAD, BLK), jnp.int32),
            pltpu.VMEM((8, BLK), jnp.int32),
            pltpu.SMEM((8, BLK), jnp.int32),
            pltpu.SMEM((2, BLK), jnp.int32),
            pltpu.SemaphoreType.DMA((2,)),
        ],
        compiler_params=pltpu.CompilerParams(vmem_limit_bytes=24 * MIB),
        name="product",
    )(rows, cols)


def totals_kernel(sums_ref, out_ref, slots, send_sems, recv_sems):
    row, col, layer = (lax.axis_index(a) for a in ("row", "col", "layer"))
    barrier = pltpu.get_barrier_semaphore()
    peers = [((row + s) % 8, col, layer) for s in range(1, 8)]
    for peer in peers:
        pl.semaphore_signal(barrier, inc=1, device_id=peer, device_id_type=MESH)
    slots[row] = sums_ref[...]
    pl.semaphore_wait(barrier, 7)
    copies = [
        pltpu.make_async_remote_copy(
            src_ref=slots.at[row],
            dst_ref=slots.at[row],
            send_sem=send_sems.at[s],
            recv_sem=recv_sems.at[s],
            device_id=peer,
            device_id_type=MESH,
        )
        for s, peer in enumerate(peers)
    ]
    for copy in copies:
        copy.start()
    for copy in copies:
        copy.wait()
    total = slots[0]
    for q in range(1, 8):
        total = total + slots[q]
    out_ref[...] = jnp.sum(total, axis=0, keepdims=True)


def reduce_totals(sums):
    return pl.pallas_call(
        totals_kernel,
        out_shape=jax.ShapeDtypeStruct((1, sums.shape[1]), jnp.float32),
        in_specs=[pl.BlockSpec(memory_space=pltpu.VMEM)],
        out_specs=pl.BlockSpec(memory_space=pltpu.VMEM),
        scratch_shapes=[
            pltpu.VMEM((8,) + sums.shape, jnp.float32),
            pltpu.SemaphoreType.DMA((7,)),
            pltpu.SemaphoreType.DMA((7,)),
        ],
        compiler_params=pltpu.CompilerParams(
            collective_id=1, has_side_effects=True, vmem_limit_bytes=4 * MIB
        ),
        name="totals",
    )(sums)


def scale_kernel(scaling, value_ref, total_ref, out_ref):
    out_ref[...] = scaling * value_ref[...] / total_ref[...]


def scale(value, total, scaling, steps=6):
    rows, lanes = value.shape
    return pl.pallas_call(
        functools.partial(scale_kernel, scaling),
        grid=(steps,),
        out_shape=jax.ShapeDtypeStruct(value.shape, jnp.float32),
        in_specs=[
            pl.BlockSpec((rows // steps, lanes), lambda i: (i, 0)),
            pl.BlockSpec((1, lanes), lambda i: (0, 0)),
        ],
        out_specs=pl.BlockSpec((rows // steps, lanes), lambda i: (i, 0)),
        compiler_params=pltpu.CompilerParams(vmem_limit_bytes=16 * MIB),
        name="scale",
    )(value, total)


def body(similarity, block_mask):
    share = pack(block_mask, similarity)
    rows, cols = gather(share)
    value, sums = product(rows, cols, *similarity.shape)
    total = reduce_totals(sums)
    scaling = similarity.shape[0] * lax.axis_size("row")
    return scale(value, total, float(scaling))


def solution(mesh):
    return jax.shard_map(
        body,
        mesh=mesh,
        in_specs=(P("row", ("col", "layer")), P("row", ("col", "layer"))),
        out_specs=P("row", ("col", "layer")),
        check_vma=False,
    )
```

time: 701 us -> 92.3 us (0.13)
  waiting for transfers between devices: 610 us -> 0 us
  Pallas kernels: 0 us -> 89.3 us
  matrix products: 37.8 us -> 0 us
  blocking collectives: 24.2 us -> 0 us
  between operations: 13.1 us -> 0.03 us
  other arithmetic: 10 us -> 0 us
    all_gather x3 -> x0, waiting for transfers between devices: 590 us -> none  [the longest x1 365 us: body(): lax.all_gather(masked, 'col', axis=1, tiled=True)]
    pallas_call x0 -> x5, Pallas kernels: none -> 89.3 us  [the longest x1 48.5 us: gather(): pl.pallas_call(gather_kernel, out_shape=[pltpu.VMEM((16, SHARE, BLK), sha...]
    dot_general x1 -> x0, matrix products: 37.8 us -> none  [body(): jnp.dot(lax.all_gather(masked, 'col', axis=1, tiled=True), inner_panel, p...]
    psum x1 -> x0, blocking collectives: 24.2 us -> none  [body(): totals = lax.psum(jnp.sum(inflated, axis=0), 'row')]
    reduce_scatter x1 -> x0, waiting for transfers between devices: 18.7 us -> none  [body(): lax.psum_scatter(partial_value, 'layer', scatter_dimension=1, tiled=True)]
  transfers between devices with their start and end apart: 4 -> 0, of which waited for: 4 -> 0; matrix products, arithmetic and copies ran while one was open for 0% -> 0% of each run, Pallas kernels for 0% -> 0%
where the time goes in v1:
time: 92.3 us; the launch traced here: 91.8 us
  Pallas kernels  89.3 us (97%)
  local copies, waits for them, and re-layouts  2.44 us (3%)
    pallas_call x1, Pallas kernels, gather(): pl.pallas_call(gather_kernel, out_shape=[pltpu.VMEM((16, SHARE, BLK), sha...  48.5 us
    pallas_call x1, Pallas kernels, product(): pl.pallas_call(product_kernel, out_shape=[pltpu.VMEM((out_rows, lanes), j...  24.5 us
    pallas_call x1, Pallas kernels, reduce_totals(): pl.pallas_call(totals_kernel, out_shape=jax.ShapeDtypeStruct((1, sums.sha...  11.4 us
    pallas_call x1, Pallas kernels, scale(): pl.pallas_call(functools.partial(scale_kernel, scaling), grid=(steps,), o...  3.1 us
    unnamed x3, local copies, waits for them, and re-layouts  2.44 us

profile of v1, /device:TPU:0, one launch (start us, length us, event | category | flops | bytes accessed | tf_op | source)
XLA Modules:
  0.0 91.8 jit_solution(14258987608706816661)
XLA Ops:
  0.0 0.8 copy.3.mask_ref
  0.8 0.0 copy-start
  0.8 1.7 %copy-done = bf16[1536,768]{1,0:T(8,128)(2,1)S(1)} copy-done((bf16[1536,768]{1,0:T(8,128)(2,1)S(1)}, bf16[1536,768]{1,0:T(8,128)(2,1)}, u32[]{:S(2)}) %copy-start) | copy-done | bytes 2359320
  2.4 1.7 %pack.1.share_ref = bf16[2320,128]{1,0:T(8,128)(2,1)S(1)} custom-call(s32[12,6]{1,0:T(8,128)S(1)} %copy.3.mask_ref, bf16[1536,768]{1,0:T(8,128)(2,1)S(1)} %copy-done), custom_call_target="tpu_custom_call" | custom-call | tf_op jit(solution)/shard_map/pack/pallas_call | solution.py:62
  4.2 48.5 %gather.1 = (bf16[16,2320,128]{2,1,0:T(8,128)(2,1)S(1)}, bf16[8,2320,128]{2,1,0:T(8,128)(2,1)S(1)}) custom-call(bf16[2320,128]{1,0:T(8,128)(2,1)S(1)} %pack.1.share_ref), custom_call_target="tpu_custom_call" | custom-call | tf_op jit(solution)/shard_map/gather/pallas_call | solution.py:255
  52.7 24.5 %product.1 = (f32[1536,768]{1,0:T(8,128)S(1)}, f32[8,768]{1,0:T(8,128)S(1)}) custom-call(bf16[16,2320,128]{2,1,0:T(8,128)(2,1)S(1)} %get-tuple-element.9.r_ref, bf16[8,2320,128]{2,1,0:T(8,128)(2,1)S(1)} %get-tuple-element.10.c_ref), custom_call_target="tpu_custom_call" | custom-call | tf_op jit(solution)/shard_map/product/pallas_call | solution.py:362
  77.3 11.4 %totals.1.total_ref = f32[1,768]{1,0:T(1,128)S(1)} custom-call(f32[8,768]{1,0:T(8,128)S(1)} %get-tuple-element.12.sums_ref), custom_call_target="tpu_custom_call" | custom-call | tf_op jit(solution)/shard_map/totals/pallas_call | solution.py:414
  88.7 3.1 %scale.1 = f32[1536,768]{1,0:T(8,128)} custom-call(f32[1536,768]{1,0:T(8,128)S(1)} %get-tuple-element.11.value_ref, f32[1,768]{1,0:T(1,128)S(1)} %totals.1.total_ref), custom_call_target="tpu_custom_call" | custom-call | tf_op jit(solution)/shard_map/scale/pallas_call | solution.py:437
Async XLA Ops:
  0.8 1.7 %copy-start = (bf16[1536,768]{1,0:T(8,128)(2,1)S(1)}, bf16[1536,768]{1,0:T(8,128)(2,1)}, u32[]{:S(2)}) copy-start(bf16[1536,768]{1,0:T(8,128)(2,1)} %x_ref.1) | copy-start | bytes 7077892

commit v2 on v1

--- a/solution.py
+++ b/solution.py
@@ -9,7 +9,7 @@
 
 BLK = 128
 MAXNZ = 18
-HEAD = 16
+HEAD = 32
 HALF = MAXNZ // 2
 SHARE = HEAD + MAXNZ * BLK
 CUT = HEAD + HALF * BLK
@@ -18,15 +18,17 @@
 
 
 def pack_kernel(mask_ref, x_ref, share_ref, sems):
-    rows, cols = mask_ref.shape
-    base = (2 * lax.axis_index("col") + lax.axis_index("layer")) * cols
+    cols, rows = mask_ref.shape
     sub = lax.broadcasted_iota(jnp.int32, (HEAD, BLK), 0)
     lane = lax.broadcasted_iota(jnp.int32, (HEAD, BLK), 1)
+    lane_row = (lane * 43) >> 8
+    lane_col = lane - lane_row * cols
 
     def one_row(i, carry):
         count, head = carry
+        below = 8 + jnp.where(i < cols, i, i - cols + 8)
         for j in range(cols):
-            here = mask_ref[i, j]
+            here = mask_ref[j, i]
 
             @pl.when(here > 0)
             def _():
@@ -36,16 +38,15 @@
                     sems.at[count],
                 ).start()
 
-            cell = (sub == i) & (lane == base + j)
-            place = (sub == rows) & (lane == count)
+            cell = ((sub == j) & (lane_row == i)) | ((sub == below) & (lane_col == j))
             head = jnp.where(cell & (here > 0), count + 1, head)
-            head = jnp.where(place & (here > 0), i * cols + j + 1, head)
             count = count + here
         return count, head
 
     count, head = lax.fori_loop(
         0, rows, one_row, (jnp.int32(0), jnp.zeros((HEAD, BLK), jnp.int32))
     )
+    head = jnp.where(lane < rows * cols, head, 0)
     share_ref[pl.ds(0, HEAD), :] = head.astype(jnp.float32).astype(share_ref.dtype)
     for s in range(MAXNZ):
 
@@ -64,13 +65,13 @@
         out_shape=pltpu.VMEM((SHARE, BLK), similarity.dtype),
         in_specs=[
             pl.BlockSpec(memory_space=pltpu.SMEM),
-            pl.BlockSpec(memory_space=pltpu.HBM),
+            pl.BlockSpec(memory_space=pl.ANY),
         ],
         out_specs=pl.BlockSpec(memory_space=pltpu.VMEM),
         scratch_shapes=[pltpu.SemaphoreType.DMA((MAXNZ,))],
-        compiler_params=pltpu.CompilerParams(vmem_limit_bytes=4 * MIB),
+        compiler_params=pltpu.CompilerParams(vmem_limit_bytes=56 * MIB),
         name="pack",
-    )(block_mask, similarity)
+    )(block_mask.T, similarity)
 
 
 def gather_kernel(share_ref, rows_ref, cols_ref, send_sems, recv_sems, own_sems):
@@ -273,89 +274,101 @@
 
 
 GROUP = 4
-
-
-def product_kernel(
-    r_ref, c_ref, out_ref, sums_ref, dense, head_v, head_s, place_v, place_s, lists, sems
-):
+DEPTH = 16
+
+
+def product_kernel(r_ref, c_ref, out_ref, sums_ref, table_v, table_s, sem):
     tiles, lanes = out_ref.shape[0] // BLK, out_ref.shape[1]
     wide = lanes // BLK
-    head = r_ref[0, pl.ds(0, HEAD), :].astype(jnp.float32)
-    for s in range(1, 16):
-        head = head + r_ref[s, pl.ds(0, HEAD), :].astype(jnp.float32)
-    head_v[...] = head.astype(jnp.int32)
+    col = lax.axis_index("col")
+
+    hr, hc = [], []
+    for q in range(16):
+        hr.append(r_ref[q, pl.ds(0, HEAD), :].astype(jnp.float32)[0:8])
     for q in range(8):
-        top = c_ref[q, pl.ds(0, HEAD), :].astype(jnp.float32).astype(jnp.int32)
-        place_v[pl.ds(q, 1), :] = top[tiles : tiles + 1, :]
-    copies = [
-        pltpu.make_async_copy(head_v, head_s, sems.at[0]),
-        pltpu.make_async_copy(place_v, place_s, sems.at[1]),
-    ]
-    for copy in copies:
+        top = c_ref[q, pl.ds(0, HEAD), :].astype(jnp.float32)
+        hc += [top[8:16], top[16:24]]
+    hr, hc = jnp.concatenate(hr, 0), jnp.concatenate(hc, 0)
+    both = (hr > 0) & (hc > 0)
+    line = lax.broadcasted_iota(jnp.int32, (BLK, BLK), 0)
+    rank = jnp.dot(
+        (line > lax.broadcasted_iota(jnp.int32, (BLK, BLK), 1)).astype(jnp.bfloat16),
+        both.astype(jnp.float32).astype(jnp.bfloat16),
+        preferred_element_type=jnp.float32,
+    )
+    rank = jnp.where(both, rank, -1.0).astype(jnp.int32)
+    place_r = (line >> 3) * SHARE + (HEAD - BLK) + hr.astype(jnp.int32) * BLK
+    place_c = (line >> 4) * SHARE + (HEAD - BLK) + hc.astype(jnp.int32) * BLK
+    count = jnp.sum(both.astype(jnp.int32), axis=0, keepdims=True)
+    most = jnp.max(count)
+    idle_c = col * SHARE + HEAD
+
+    def fill(done):
+        for p in range(DEPTH):
+            at = rank == done + p
+            some = count > done + p
+            first = jnp.sum(jnp.where(at, place_r, 0), axis=0, keepdims=True)
+            second = jnp.sum(jnp.where(at, place_c, 0), axis=0, keepdims=True)
+            table_v[pl.ds(p, 1), :] = jnp.where(some, first, HEAD)
+            table_v[pl.ds(DEPTH + p, 1), :] = jnp.where(some, second, idle_c)
+        table_v[pl.ds(2 * DEPTH, 1), :] = jnp.clip(count - done, 0, DEPTH)
+        copy = pltpu.make_async_copy(table_v, table_s, sem)
         copy.start()
-
-    @pl.loop(0, dense.shape[0] // 256)
-    def _(t):
-        dense[pl.ds(pl.multiple_of(t * 256, 256), 256), :] = jnp.zeros((256, lanes), dense.dtype)
-
-    for copy in copies:
         copy.wait()
 
-    @pl.loop(0, 8)
-    def _(q):
-        @pl.loop(0, MAXNZ)
-        def _(s):
-            v = place_s[q, s] - 1
-
-            @pl.when(v >= 0)
-            def _():
-                k = q * tiles + v // wide
-                j = v % wide
-                dense[
-                    pl.ds(pl.multiple_of(k * BLK, BLK), BLK),
-                    pl.ds(pl.multiple_of(j * BLK, BLK), BLK),
-                ] = c_ref[q, pl.ds(pl.multiple_of(HEAD + s * BLK, HEAD), BLK), :]
-
-    sums_ref[...] = jnp.zeros(sums_ref.shape, jnp.float32)
+    def part(i, j, g):
+        cell = i * wide + j
+        left, right = [], []
+        have = table_s[2 * DEPTH, cell]
+        for t in range(GROUP):
+            p = g * GROUP + t
+            a = r_ref[pl.ds(pl.multiple_of(table_s[p, cell], HEAD), BLK), :]
+            left.append(jnp.where(p < have, a, jnp.zeros_like(a)))
+            right.append(c_ref[pl.ds(pl.multiple_of(table_s[DEPTH + p, cell], HEAD), BLK), :])
+        return jnp.dot(
+            jnp.concatenate(left, 1),
+            jnp.concatenate(right, 0),
+            preferred_element_type=jnp.float32,
+        )
+
+    def more(i, j, first):
+        here = pl.ds(pl.multiple_of(i * BLK, BLK), BLK)
+
+        @pl.loop(first, (table_s[2 * DEPTH, i * wide + j] + GROUP - 1) // GROUP)
+        def _(g):
+            out_ref[here, pl.ds(j * BLK, BLK)] += part(i, j, g)
+
+    fill(0)
+    r_ref = r_ref.reshape(16 * SHARE, BLK)
+    c_ref = c_ref.reshape(8 * SHARE, BLK)
 
     @pl.loop(0, tiles)
     def _(i):
-        def look(k, count):
-            v = head_s[i, k]
-            lists[0, count] = k
-            lists[1, count] = v - 1
-            return count + jnp.where(v > 0, 1, 0)
-
-        count = lax.fori_loop(0, 8 * tiles, look, jnp.int32(0), unroll=8)
-        for t in range(GROUP):
-            lists[0, count + t] = 0
-            lists[1, count + t] = 0
         here = pl.ds(pl.multiple_of(i * BLK, BLK), BLK)
-
-        def part(g):
-            left, right = [], []
-            for t in range(GROUP):
-                p = g * GROUP + t
-                k, v = lists[0, p], lists[1, p]
-                a = r_ref[k // wide, pl.ds(pl.multiple_of(HEAD + v * BLK, HEAD), BLK), :]
-                left.append(jnp.where(p < count, a, jnp.zeros_like(a)))
-                right.append(dense[pl.ds(pl.multiple_of(k * BLK, BLK), BLK), :])
-            return jnp.dot(
-                jnp.concatenate(left, 1),
-                jnp.concatenate(right, 0),
-                preferred_element_type=jnp.float32,
-            )
-
-        out_ref[here, :] = part(0)
-
-        @pl.loop(1, (count + GROUP - 1) // GROUP)
-        def _(g):
-            out_ref[here, :] += part(g)
-
+        for j in range(wide):
+            out_ref[here, pl.ds(j * BLK, BLK)] = part(i, j, 0)
+        for j in range(wide):
+            more(i, j, 1)
+
+    @pl.loop(1, (most + DEPTH - 1) // DEPTH)
+    def _(d):
+        fill(d * DEPTH)
+
+        @pl.loop(0, tiles)
+        def _(i):
+            for j in range(wide):
+                more(i, j, 0)
+
+    def square(t, total):
+        here = pl.ds(pl.multiple_of(t * 64, 64), 64)
         value = out_ref[here, :]
         value = value * value
         out_ref[here, :] = value
-        sums_ref[...] += jnp.sum(value.reshape(BLK // 8, 8, lanes), axis=0)
+        return total + jnp.sum(value.reshape(8, 8, lanes), axis=0)
+
+    sums_ref[...] = lax.fori_loop(
+        0, tiles * BLK // 64, square, jnp.zeros((8, lanes), jnp.float32)
+    )
 
 
 def product(rows, cols, out_rows, lanes):
@@ -368,15 +381,11 @@
         in_specs=[pl.BlockSpec(memory_space=pltpu.VMEM)] * 2,
         out_specs=[pl.BlockSpec(memory_space=pltpu.VMEM)] * 2,
         scratch_shapes=[
-            pltpu.VMEM((8 * out_rows, lanes), rows.dtype),
-            pltpu.VMEM((HEAD, BLK), jnp.int32),
-            pltpu.SMEM((HEAD, BLK), jnp.int32),
-            pltpu.VMEM((8, BLK), jnp.int32),
-            pltpu.SMEM((8, BLK), jnp.int32),
-            pltpu.SMEM((2, BLK), jnp.int32),
-            pltpu.SemaphoreType.DMA((2,)),
-        ],
-        compiler_params=pltpu.CompilerParams(vmem_limit_bytes=24 * MIB),
+            pltpu.VMEM((2 * DEPTH + 8, BLK), jnp.int32),
+            pltpu.SMEM((2 * DEPTH + 8, BLK), jnp.int32),
+            pltpu.SemaphoreType.DMA(()),
+        ],
+        compiler_params=pltpu.CompilerParams(vmem_limit_bytes=8 * MIB),
         name="product",
     )(rows, cols)
 
@@ -428,21 +437,34 @@
     )(sums)
 
 
-def scale_kernel(scaling, value_ref, total_ref, out_ref):
-    out_ref[...] = scaling * value_ref[...] / total_ref[...]
-
-
-def scale(value, total, scaling, steps=6):
+STEPS = 6
+
+
+def scale_kernel(scaling, value_ref, total_ref, out_ref, staged, sems):
+    step = staged.shape[1]
+    total = total_ref[...]
+    copies = []
+    for t in range(STEPS):
+        here = pl.ds(t * step, step)
+        staged[t] = scaling * value_ref[here, :] / total
+        copy = pltpu.make_async_copy(staged.at[t], out_ref.at[here], sems.at[t])
+        copy.start()
+        copies.append(copy)
+    for copy in copies:
+        copy.wait()
+
+
+def scale(value, total, scaling):
     rows, lanes = value.shape
     return pl.pallas_call(
         functools.partial(scale_kernel, scaling),
-        grid=(steps,),
         out_shape=jax.ShapeDtypeStruct(value.shape, jnp.float32),
-        in_specs=[
-            pl.BlockSpec((rows // steps, lanes), lambda i: (i, 0)),
-            pl.BlockSpec((1, lanes), lambda i: (0, 0)),
-        ],
-        out_specs=pl.BlockSpec((rows // steps, lanes), lambda i: (i, 0)),
+        in_specs=[pl.BlockSpec(memory_space=pltpu.VMEM)] * 2,
+        out_specs=pl.BlockSpec(memory_space=pltpu.HBM),
+        scratch_shapes=[
+            pltpu.VMEM((STEPS, rows // STEPS, lanes), jnp.float32),
+            pltpu.SemaphoreType.DMA((STEPS,)),
+        ],
         compiler_params=pltpu.CompilerParams(vmem_limit_bytes=16 * MIB),
         name="scale",
     )(value, total)

time: 92.3 us -> 72.2 us (0.78)
  Pallas kernels: 89.3 us -> 71.3 us
  local copies, waits for them, and re-layouts: 2.44 us -> 0 us
    pallas_call x1, Pallas kernels: 24.5 us -> 7.79 us  [product(): pl.pallas_call(product_kernel, out_shape=[pltpu.VMEM((out_rows, lanes), j...]
    unnamed x3 -> x0, local copies, waits for them, and re-layouts: 2.44 us -> none
where the time goes in v2:
time: 72.2 us; the launch traced here: 71.3 us
  Pallas kernels  71.3 us (99%)
    pallas_call x1, Pallas kernels, gather(): pl.pallas_call(gather_kernel, out_shape=[pltpu.VMEM((16, SHARE, BLK), sha...  48.6 us
    pallas_call x1, Pallas kernels, reduce_totals(): pl.pallas_call(totals_kernel, out_shape=jax.ShapeDtypeStruct((1, sums.sha...  10.5 us
    pallas_call x1, Pallas kernels, product(): pl.pallas_call(product_kernel, out_shape=[pltpu.VMEM((out_rows, lanes), j...  7.79 us
    pallas_call x1, Pallas kernels, scale(): pl.pallas_call(functools.partial(scale_kernel, scaling), out_shape=jax.Sh...  2.28 us
    pallas_call x1, Pallas kernels, pack(): pl.pallas_call(pack_kernel, out_shape=pltpu.VMEM((SHARE, BLK), similarity...  2.12 us

profile of v2, /device:TPU:0, one launch (start us, length us, event | category | flops | bytes accessed | tf_op | source)
XLA Modules:
  0.0 71.3 jit_solution(11830458622738778048)
XLA Ops:
  0.0 2.1 %pack.1.share_ref = bf16[2336,128]{1,0:T(8,128)(2,1)S(1)} custom-call(s32[6,12]{1,0:T(8,128)} %bitcast.1, bf16[1536,768]{1,0:T(8,128)(2,1)} %x_ref.1), custom_call_target="tpu_custom_call" | custom-call | tf_op jit(solution)/shard_map/pack/pallas_call | solution.py:63
  2.1 48.6 %gather.1 = (bf16[16,2336,128]{2,1,0:T(8,128)(2,1)S(1)}, bf16[8,2336,128]{2,1,0:T(8,128)(2,1)S(1)}) custom-call(bf16[2336,128]{1,0:T(8,128)(2,1)S(1)} %pack.1.share_ref), custom_call_target="tpu_custom_call" | custom-call | tf_op jit(solution)/shard_map/gather/pallas_call | solution.py:256
  50.8 7.8 %product.1 = (f32[1536,768]{1,0:T(8,128)S(1)}, f32[8,768]{1,0:T(8,128)S(1)}) custom-call(bf16[16,2336,128]{2,1,0:T(8,128)(2,1)S(1)} %get-tuple-element.9.r_ref, bf16[8,2336,128]{2,1,0:T(8,128)(2,1)S(1)} %get-tuple-element.10.c_ref), custom_call_target="tpu_custom_call" | custom-call | tf_op jit(solution)/shard_map/product/pallas_call | solution.py:375
  58.6 10.5 %totals.1.total_ref = f32[1,768]{1,0:T(1,128)S(1)} custom-call(f32[8,768]{1,0:T(8,128)S(1)} %get-tuple-element.12.sums_ref), custom_call_target="tpu_custom_call" | custom-call | tf_op jit(solution)/shard_map/totals/pallas_call | solution.py:423
  69.1 2.3 %scale.1 = f32[1536,768]{1,0:T(8,128)} custom-call(f32[1536,768]{1,0:T(8,128)S(1)} %get-tuple-element.11.value_ref, f32[1,768]{1,0:T(1,128)S(1)} %totals.1.total_ref), custom_call_target="tpu_custom_call" | custom-call | tf_op jit(solution)/shard_map/scale/pallas_call | solution.py:459

commit v3 on v2

--- a/solution.py
+++ b/solution.py
@@ -12,7 +12,6 @@
 HEAD = 32
 HALF = MAXNZ // 2
 SHARE = HEAD + MAXNZ * BLK
-CUT = HEAD + HALF * BLK
 MIB = 1 << 20
 MESH = pl.DeviceIdType.MESH
 
@@ -74,7 +73,18 @@
     )(block_mask.T, similarity)
 
 
-def gather_kernel(share_ref, rows_ref, cols_ref, send_sems, recv_sems, own_sems):
+LAST = 5
+SPLIT = 7
+
+
+def span(first, last):
+    low = HEAD + first * BLK if first else 0
+    return pl.ds(low, HEAD + last * BLK - low)
+
+
+def gather_kernel(
+    share_ref, rows_ref, cols_ref, relay, send_sems, recv_sems, own_sems
+):
     row, col, layer = (lax.axis_index(a) for a in ("row", "col", "layer"))
     high, x = row // 4, row % 4
     z, low = col // 2, col % 2
@@ -103,19 +113,20 @@
         pltpu.make_async_copy(share_ref, rows_ref.at[mine], own_sems.at[0]),
         pltpu.make_async_copy(share_ref, cols_ref.at[row], own_sems.at[1]),
     ]
-    for copy in keep:
-        copy.start()
-
-    H1, H2, ALL = pl.ds(0, CUT), pl.ds(CUT, SHARE - CUT), pl.ds(0, SHARE)
-    n = [0]
+
+    EARLY = MAXNZ - LAST
+    ALL = span(0, MAXNZ)
+    H1, H2 = span(0, HALF), span(HALF, MAXNZ)
+    U1, U2, U, L = span(0, SPLIT), span(SPLIT, EARLY), span(0, EARLY), span(EARLY, MAXNZ)
+    T = pl.ds(0, LAST * BLK)
     started = []
-
-    def send(src, dst, part, peer):
-        k = n[0]
-        n[0] += 1
+    waited = set()
+
+    def send(src, dst, part, peer, into=None):
+        k = len(started)
         copy = pltpu.make_async_remote_copy(
             src_ref=src.at[part],
-            dst_ref=dst.at[part],
+            dst_ref=dst.at[part if into is None else into],
             send_sem=send_sems.at[k],
             recv_sem=recv_sems.at[k],
             device_id=peer,
@@ -124,8 +135,6 @@
         copy.start()
         started.append(copy)
         return k
-
-    waited = set()
 
     def arrived(k, dst, part, peer):
         waited.add(k)
@@ -138,38 +147,45 @@
             device_id_type=MESH,
         ).wait_recv()
 
-    def r(c):
-        return rows_ref.at[2 * c + layer]
-
-    def rsib(c):
-        return rows_ref.at[2 * c + 1 - layer]
+    def other(q):
+        return q + 1 - 2 * (q % 2)
+
+    def r(q):
+        return rows_ref.at[2 * q + layer]
+
+    def rsib(q):
+        return rows_ref.at[2 * q + 1 - layer]
 
     def c(q):
         return cols_ref.at[q]
 
+    def across(q):
+        return c((q + 4) % 8)
+
     own_r, own_c = r(col), c(row)
-    lo1 = send(share_ref, own_r, H1, lo)
+    y_r, y_c = r(mate), c(far)
+    zm_r, zp_r, zz_r = (r(along_z(s)) for s in (3, 1, 2))
+    ym_r, yp_r, yy_r = (r(other(along_z(s))) for s in (3, 1, 2))
+    xm_c, xp_c, xx_c = (c(along_x(s)) for s in (3, 1, 2))
+    ym_c, yp_c, yy_c = (across(along_x(s)) for s in (3, 1, 2))
+
+    lo1 = send(share_ref, own_r, U1, lo)
     zp1 = send(share_ref, own_r, H1, zp)
     zm2 = send(share_ref, own_r, H2, zm)
     xp1 = send(share_ref, own_c, H1, xp)
     xm2 = send(share_ref, own_c, H2, xm)
-    lo2 = send(share_ref, own_r, H2, lo)
+    lo2 = send(share_ref, own_r, U2, lo)
     zp2 = send(share_ref, own_r, H2, zp)
     zm1 = send(share_ref, own_r, H1, zm)
     xp2 = send(share_ref, own_c, H2, xp)
     xm1 = send(share_ref, own_c, H1, xm)
+    lo3 = send(share_ref, own_r, L, lo)
     sb0 = send(share_ref, own_r, ALL, sib)
-
-    y_r = r(mate)
-    arrived(lo1, y_r, H1, lo)
-    hi1 = send(y_r, c(row), H1, hi)
-    yzp1 = send(y_r, y_r, H1, zp)
-    arrived(lo2, y_r, H2, lo)
-    hi2 = send(y_r, c(row), H2, hi)
-    yzm2 = send(y_r, y_r, H2, zm)
-
-    zm_r, zp_r, zz_r = r(along_z(3)), r(along_z(1)), r(along_z(2))
-    xm_c, xp_c, xx_c = c(along_x(3)), c(along_x(1)), c(along_x(2))
+    for copy in keep:
+        copy.start()
+
+    arrived(lo1, y_r, U1, lo)
+    hi1 = send(y_r, own_c, U1, hi)
     arrived(zp1, zm_r, H1, zm)
     fzp = send(zm_r, zm_r, H1, zp)
     arrived(zm2, zp_r, H2, zp)
@@ -178,78 +194,94 @@
     fxp = send(xm_c, xm_c, H1, xp)
     arrived(xm2, xp_c, H2, xp)
     fxm = send(xp_c, xp_c, H2, xm)
-    yzp2 = send(y_r, y_r, H2, zp)
-    yzm1 = send(y_r, y_r, H1, zm)
+    lzp = send(zp_r, zp_r, L, lo)
+    txp = send(xp_c, relay.at[0], L, lo, T)
+    yzp1 = send(y_r, y_r, U1, zp)
+    arrived(lo2, y_r, U2, lo)
+    hi2 = send(y_r, own_c, U2, hi)
+    yzm2 = send(y_r, y_r, U2, zm)
+    yzp2 = send(y_r, y_r, U2, zp)
+    yzm1 = send(y_r, y_r, U1, zm)
+    arrived(hi1, y_c, U1, hi)
+    yxp1 = send(y_c, y_c, U1, xp)
+    arrived(lo3, y_r, L, lo)
+    hi3 = send(y_r, own_c, L, hi)
     sb1 = send(y_r, y_r, ALL, sib)
 
-    y_c = c(far)
-    arrived(hi1, y_c, H1, hi)
-    yxp1 = send(y_c, y_c, H1, xp)
-    arrived(hi2, y_c, H2, hi)
-    yxm2 = send(y_c, y_c, H2, xm)
-    yxp2 = send(y_c, y_c, H2, xp)
-    yxm1 = send(y_c, y_c, H1, xm)
-
-    def other(q):
-        return q + 1 - 2 * (q % 2)
-
-    ym_r, yp_r, yy_r = (r(other(along_z(s))) for s in (3, 1, 2))
-    arrived(yzp1, ym_r, H1, zm)
-    gzp = send(ym_r, ym_r, H1, zp)
-    arrived(yzm2, yp_r, H2, zp)
-    gzm = send(yp_r, yp_r, H2, zm)
-
-    def across(q):
-        return c((q + 4) % 8)
-
-    ym_c, yp_c, yy_c = (across(along_x(s)) for s in (3, 1, 2))
-    arrived(yxp1, ym_c, H1, xm)
-    gxp = send(ym_c, ym_c, H1, xp)
-    arrived(yxm2, yp_c, H2, xp)
-    gxm = send(yp_c, yp_c, H2, xm)
-
     arrived(zp2, zm_r, H2, zm)
+    lzm = send(zm_r, zm_r, L, lo)
     sb2 = send(zm_r, zm_r, ALL, sib)
+    arrived(xp2, xm_c, H2, xm)
+    txm = send(xm_c, relay.at[1], L, lo, T)
     arrived(zm1, zp_r, H1, zp)
     sb3 = send(zp_r, zp_r, ALL, sib)
+    arrived(hi2, y_c, U2, hi)
+    yxm2 = send(y_c, y_c, U2, xm)
+    yxp2 = send(y_c, y_c, U2, xp)
+    yxm1 = send(y_c, y_c, U1, xm)
+    arrived(txp, relay.at[0], T, lo)
+    uxp = send(relay.at[0], xp_c, T, hi, L)
+    arrived(fzm, zz_r, H2, zp)
+    lzz = send(zz_r, zz_r, L, lo)
+    arrived(fxm, xx_c, H2, xp)
+    txx = send(xx_c, relay.at[2], L, lo, T)
     arrived(fzp, zz_r, H1, zm)
-    arrived(fzm, zz_r, H2, zp)
     sb4 = send(zz_r, zz_r, ALL, sib)
-    arrived(yzp2, ym_r, H2, zm)
-    sb5 = send(ym_r, ym_r, ALL, sib)
-    arrived(yzm1, yp_r, H1, zp)
-    sb6 = send(yp_r, yp_r, ALL, sib)
-    arrived(gzp, yy_r, H1, zm)
-    sb7 = send(yy_r, yy_r, H1, sib)
-    arrived(gzm, yy_r, H2, zp)
-    sb8 = send(yy_r, yy_r, H2, sib)
-
-    arrived(xp2, xm_c, H2, xm)
+    arrived(txm, relay.at[1], T, lo)
+    uxm = send(relay.at[1], xm_c, T, hi, L)
+
+    arrived(yzp1, ym_r, U1, zm)
+    gzp = send(ym_r, ym_r, U1, zp)
+    arrived(yzm2, yp_r, U2, zp)
+    gzm = send(yp_r, yp_r, U2, zm)
+    arrived(yxp1, ym_c, U1, xm)
+    gxp = send(ym_c, ym_c, U1, xp)
+    arrived(yxm2, yp_c, U2, xp)
+    gxm = send(yp_c, yp_c, U2, xm)
+    arrived(lzp, yp_r, L, lo)
+    arrived(yzm1, yp_r, U1, zp)
+    sb5 = send(yp_r, yp_r, ALL, sib)
+    arrived(txx, relay.at[2], T, lo)
+    uxx = send(relay.at[2], xx_c, T, hi, L)
+    arrived(yzp2, ym_r, U2, zm)
+    arrived(lzm, ym_r, L, lo)
+    sb6 = send(ym_r, ym_r, ALL, sib)
+    arrived(lzz, yy_r, L, lo)
+    sb7 = send(yy_r, yy_r, L, sib)
+    arrived(gzp, yy_r, U1, zm)
+    sb8 = send(yy_r, yy_r, U1, sib)
+    arrived(gzm, yy_r, U2, zp)
+    sb9 = send(yy_r, yy_r, U2, sib)
+
+    arrived(hi3, y_c, L, hi)
     arrived(xm1, xp_c, H1, xp)
     arrived(fxp, xx_c, H1, xm)
-    arrived(fxm, xx_c, H2, xp)
-    arrived(yxp2, ym_c, H2, xm)
-    arrived(yxm1, yp_c, H1, xp)
-    arrived(gxp, yy_c, H1, xm)
-    arrived(gxm, yy_c, H2, xp)
+    arrived(yxp2, ym_c, U2, xm)
+    arrived(yxm1, yp_c, U1, xp)
+    arrived(uxp, yp_c, L, hi)
+    arrived(uxm, ym_c, L, hi)
+    arrived(uxx, yy_c, L, hi)
+    arrived(gxp, yy_c, U1, xm)
+    arrived(gxm, yy_c, U2, xp)
 
     arrived(sb0, rsib(col), ALL, sib)
     arrived(sb1, rsib(mate), ALL, sib)
     arrived(sb2, rsib(along_z(3)), ALL, sib)
     arrived(sb3, rsib(along_z(1)), ALL, sib)
     arrived(sb4, rsib(along_z(2)), ALL, sib)
-    arrived(sb5, rsib(other(along_z(3))), ALL, sib)
-    arrived(sb6, rsib(other(along_z(1))), ALL, sib)
-    arrived(sb7, rsib(other(along_z(2))), H1, sib)
-    arrived(sb8, rsib(other(along_z(2))), H2, sib)
-    assert waited == set(range(n[0])) and n[0] == COPIES
+    arrived(sb5, rsib(other(along_z(1))), ALL, sib)
+    arrived(sb6, rsib(other(along_z(3))), ALL, sib)
+    arrived(sb7, rsib(other(along_z(2))), L, sib)
+    arrived(sb8, rsib(other(along_z(2))), U1, sib)
+    arrived(sb9, rsib(other(along_z(2))), U2, sib)
+    assert waited == set(range(len(started))) and len(started) == COPIES
     for copy in started:
         copy.wait_send()
     for copy in keep:
         copy.wait()
 
 
-COPIES = 37
+COPIES = 49
 
 
 def gather(share):
@@ -262,6 +294,7 @@
         in_specs=[pl.BlockSpec(memory_space=pltpu.VMEM)],
         out_specs=[pl.BlockSpec(memory_space=pltpu.VMEM)] * 2,
         scratch_shapes=[
+            pltpu.VMEM((3, LAST * BLK, BLK), share.dtype),
             pltpu.SemaphoreType.DMA((COPIES,)),
             pltpu.SemaphoreType.DMA((COPIES,)),
             pltpu.SemaphoreType.DMA((2,)),
@@ -471,8 +504,7 @@
 
 
 def body(similarity, block_mask):
-    share = pack(block_mask, similarity)
-    rows, cols = gather(share)
+    rows, cols = gather(pack(block_mask, similarity))
     value, sums = product(rows, cols, *similarity.shape)
     total = reduce_totals(sums)
     scaling = similarity.shape[0] * lax.axis_size("row")

time: 72.2 us -> 69 us (0.956)
  Pallas kernels: 71.3 us -> 68.6 us
    pallas_call x1, Pallas kernels: 48.6 us -> 46.6 us  [gather(): pl.pallas_call(gather_kernel, out_shape=[pltpu.VMEM((16, SHARE, BLK), sha...]
where the time goes in v3:
time: 69 us; the launch traced here: 68.6 us
  Pallas kernels  68.6 us (99%)
    pallas_call x1, Pallas kernels, gather(): pl.pallas_call(gather_kernel, out_shape=[pltpu.VMEM((16, SHARE, BLK), sha...  46.6 us
    pallas_call x1, Pallas kernels, reduce_totals(): pl.pallas_call(totals_kernel, out_shape=jax.ShapeDtypeStruct((1, sums.sha...  9.82 us
    pallas_call x1, Pallas kernels, product(): pl.pallas_call(product_kernel, out_shape=[pltpu.VMEM((out_rows, lanes), j...  7.77 us
    pallas_call x1, Pallas kernels, scale(): pl.pallas_call(functools.partial(scale_kernel, scaling), out_shape=jax.Sh...  2.28 us
    pallas_call x1, Pallas kernels, pack(): pl.pallas_call(pack_kernel, out_shape=pltpu.VMEM((SHARE, BLK), similarity...  2.08 us

profile of v3, /device:TPU:0, one launch (start us, length us, event | category | flops | bytes accessed | tf_op | source)
XLA Modules:
  0.0 68.6 jit_solution(2089775399056316593)
XLA Ops:
  0.0 2.1 %pack.1.share_ref = bf16[2336,128]{1,0:T(8,128)(2,1)S(1)} custom-call(s32[6,12]{1,0:T(8,128)} %bitcast.1, bf16[1536,768]{1,0:T(8,128)(2,1)} %x_ref.1), custom_call_target="tpu_custom_call" | custom-call | tf_op jit(solution)/shard_map/pack/pallas_call | solution.py:62
  2.1 46.6 %gather.1 = (bf16[16,2336,128]{2,1,0:T(8,128)(2,1)S(1)}, bf16[8,2336,128]{2,1,0:T(8,128)(2,1)S(1)}) custom-call(bf16[2336,128]{1,0:T(8,128)(2,1)S(1)} %pack.1.share_ref), custom_call_target="tpu_custom_call" | custom-call | tf_op jit(solution)/shard_map/gather/pallas_call | solution.py:288
  48.7 7.8 %product.1 = (f32[1536,768]{1,0:T(8,128)S(1)}, f32[8,768]{1,0:T(8,128)S(1)}) custom-call(bf16[16,2336,128]{2,1,0:T(8,128)(2,1)S(1)} %get-tuple-element.9.r_ref, bf16[8,2336,128]{2,1,0:T(8,128)(2,1)S(1)} %get-tuple-element.10.c_ref), custom_call_target="tpu_custom_call" | custom-call | tf_op jit(solution)/shard_map/product/pallas_call | solution.py:408
  56.5 9.8 %totals.1.total_ref = f32[1,768]{1,0:T(1,128)S(1)} custom-call(f32[8,768]{1,0:T(8,128)S(1)} %get-tuple-element.12.sums_ref), custom_call_target="tpu_custom_call" | custom-call | tf_op jit(solution)/shard_map/totals/pallas_call | solution.py:456
  66.3 2.3 %scale.1 = f32[1536,768]{1,0:T(8,128)} custom-call(f32[1536,768]{1,0:T(8,128)S(1)} %get-tuple-element.11.value_ref, f32[1,768]{1,0:T(1,128)S(1)} %totals.1.total_ref), custom_call_target="tpu_custom_call" | custom-call | tf_op jit(solution)/shard_map/scale/pallas_call | solution.py:492

commit v4 on v3

--- a/solution.py
+++ b/solution.py
@@ -117,7 +117,8 @@
     EARLY = MAXNZ - LAST
     ALL = span(0, MAXNZ)
     H1, H2 = span(0, HALF), span(HALF, MAXNZ)
-    U1, U2, U, L = span(0, SPLIT), span(SPLIT, EARLY), span(0, EARLY), span(EARLY, MAXNZ)
+    U1, U2, L = span(0, SPLIT), span(SPLIT, EARLY), span(EARLY, MAXNZ)
+    V1, V2, V3, V4 = span(0, 4), span(4, SPLIT), span(SPLIT, 10), span(10, EARLY)
     T = pl.ds(0, LAST * BLK)
     started = []
     waited = set()
@@ -186,6 +187,7 @@
 
     arrived(lo1, y_r, U1, lo)
     hi1 = send(y_r, own_c, U1, hi)
+    yzp1 = send(y_r, y_r, U1, zp)
     arrived(zp1, zm_r, H1, zm)
     fzp = send(zm_r, zm_r, H1, zp)
     arrived(zm2, zp_r, H2, zp)
@@ -194,9 +196,8 @@
     fxp = send(xm_c, xm_c, H1, xp)
     arrived(xm2, xp_c, H2, xp)
     fxm = send(xp_c, xp_c, H2, xm)
+    txp = send(xp_c, relay.at[0], L, lo, T)
     lzp = send(zp_r, zp_r, L, lo)
-    txp = send(xp_c, relay.at[0], L, lo, T)
-    yzp1 = send(y_r, y_r, U1, zp)
     arrived(lo2, y_r, U2, lo)
     hi2 = send(y_r, own_c, U2, hi)
     yzm2 = send(y_r, y_r, U2, zm)
@@ -209,10 +210,10 @@
     sb1 = send(y_r, y_r, ALL, sib)
 
     arrived(zp2, zm_r, H2, zm)
+    arrived(xp2, xm_c, H2, xm)
+    txm = send(xm_c, relay.at[1], L, lo, T)
     lzm = send(zm_r, zm_r, L, lo)
     sb2 = send(zm_r, zm_r, ALL, sib)
-    arrived(xp2, xm_c, H2, xm)
-    txm = send(xm_c, relay.at[1], L, lo, T)
     arrived(zm1, zp_r, H1, zp)
     sb3 = send(zp_r, zp_r, ALL, sib)
     arrived(hi2, y_c, U2, hi)
@@ -221,19 +222,21 @@
     yxm1 = send(y_c, y_c, U1, xm)
     arrived(txp, relay.at[0], T, lo)
     uxp = send(relay.at[0], xp_c, T, hi, L)
+    arrived(fxm, xx_c, H2, xp)
+    txx = send(xx_c, relay.at[2], L, lo, T)
     arrived(fzm, zz_r, H2, zp)
     lzz = send(zz_r, zz_r, L, lo)
-    arrived(fxm, xx_c, H2, xp)
-    txx = send(xx_c, relay.at[2], L, lo, T)
     arrived(fzp, zz_r, H1, zm)
     sb4 = send(zz_r, zz_r, ALL, sib)
     arrived(txm, relay.at[1], T, lo)
     uxm = send(relay.at[1], xm_c, T, hi, L)
 
     arrived(yzp1, ym_r, U1, zm)
-    gzp = send(ym_r, ym_r, U1, zp)
+    gzp = send(ym_r, ym_r, V1, zp)
+    gzq = send(ym_r, ym_r, V2, zp)
     arrived(yzm2, yp_r, U2, zp)
-    gzm = send(yp_r, yp_r, U2, zm)
+    gzm = send(yp_r, yp_r, V3, zm)
+    gzn = send(yp_r, yp_r, V4, zm)
     arrived(yxp1, ym_c, U1, xm)
     gxp = send(ym_c, ym_c, U1, xp)
     arrived(yxm2, yp_c, U2, xp)
@@ -248,10 +251,14 @@
     sb6 = send(ym_r, ym_r, ALL, sib)
     arrived(lzz, yy_r, L, lo)
     sb7 = send(yy_r, yy_r, L, sib)
-    arrived(gzp, yy_r, U1, zm)
-    sb8 = send(yy_r, yy_r, U1, sib)
-    arrived(gzm, yy_r, U2, zp)
-    sb9 = send(yy_r, yy_r, U2, sib)
+    arrived(gzp, yy_r, V1, zm)
+    sb8 = send(yy_r, yy_r, V1, sib)
+    arrived(gzm, yy_r, V3, zp)
+    sb9 = send(yy_r, yy_r, V3, sib)
+    arrived(gzn, yy_r, V4, zp)
+    sb10 = send(yy_r, yy_r, V4, sib)
+    arrived(gzq, yy_r, V2, zm)
+    sb11 = send(yy_r, yy_r, V2, sib)
 
     arrived(hi3, y_c, L, hi)
     arrived(xm1, xp_c, H1, xp)
@@ -272,8 +279,10 @@
     arrived(sb5, rsib(other(along_z(1))), ALL, sib)
     arrived(sb6, rsib(other(along_z(3))), ALL, sib)
     arrived(sb7, rsib(other(along_z(2))), L, sib)
-    arrived(sb8, rsib(other(along_z(2))), U1, sib)
-    arrived(sb9, rsib(other(along_z(2))), U2, sib)
+    arrived(sb8, rsib(other(along_z(2))), V1, sib)
+    arrived(sb9, rsib(other(along_z(2))), V3, sib)
+    arrived(sb10, rsib(other(along_z(2))), V4, sib)
+    arrived(sb11, rsib(other(along_z(2))), V2, sib)
     assert waited == set(range(len(started))) and len(started) == COPIES
     for copy in started:
         copy.wait_send()
@@ -281,7 +290,7 @@
         copy.wait()
 
 
-COPIES = 49
+COPIES = 53
 
 
 def gather(share):
@@ -358,10 +367,8 @@
             a = r_ref[pl.ds(pl.multiple_of(table_s[p, cell], HEAD), BLK), :]
             left.append(jnp.where(p < have, a, jnp.zeros_like(a)))
             right.append(c_ref[pl.ds(pl.multiple_of(table_s[DEPTH + p, cell], HEAD), BLK), :])
-        return jnp.dot(
-            jnp.concatenate(left, 1),
-            jnp.concatenate(right, 0),
-            preferred_element_type=jnp.float32,
+        return sum(
+            jnp.dot(a, b, preferred_element_type=jnp.float32) for a, b in zip(left, right)
         )
 
     def more(i, j, first):
@@ -375,13 +382,22 @@
     r_ref = r_ref.reshape(16 * SHARE, BLK)
     c_ref = c_ref.reshape(8 * SHARE, BLK)
 
-    @pl.loop(0, tiles)
+    @pl.loop(0, tiles, unroll=3)
     def _(i):
         here = pl.ds(pl.multiple_of(i * BLK, BLK), BLK)
         for j in range(wide):
             out_ref[here, pl.ds(j * BLK, BLK)] = part(i, j, 0)
-        for j in range(wide):
-            more(i, j, 1)
+
+    @pl.loop(0, tiles)
+    def _(i):
+        top = table_s[2 * DEPTH, i * wide]
+        for j in range(1, wide):
+            top = jnp.maximum(top, table_s[2 * DEPTH, i * wide + j])
+
+        @pl.when(top > GROUP)
+        def _():
+            for j in range(wide):
+                more(i, j, 1)
 
     @pl.loop(1, (most + DEPTH - 1) // DEPTH)
     def _(d):
@@ -399,9 +415,10 @@
         out_ref[here, :] = value
         return total + jnp.sum(value.reshape(8, 8, lanes), axis=0)
 
-    sums_ref[...] = lax.fori_loop(
+    total = lax.fori_loop(
         0, tiles * BLK // 64, square, jnp.zeros((8, lanes), jnp.float32)
     )
+    sums_ref[...] = jnp.sum(total, axis=0, keepdims=True)
 
 
 def product(rows, cols, out_rows, lanes):
@@ -409,7 +426,7 @@
         product_kernel,
         out_shape=[
             pltpu.VMEM((out_rows, lanes), jnp.float32),
-            pltpu.VMEM((8, lanes), jnp.float32),
+            pltpu.VMEM((1, lanes), jnp.float32),
         ],
         in_specs=[pl.BlockSpec(memory_space=pltpu.VMEM)] * 2,
         out_specs=[pl.BlockSpec(memory_space=pltpu.VMEM)] * 2,
@@ -425,43 +442,47 @@
 
 def totals_kernel(sums_ref, out_ref, slots, send_sems, recv_sems):
     row, col, layer = (lax.axis_index(a) for a in ("row", "col", "layer"))
+    high, x = row // 4, row % 4
+    near = [(4 * high + (x + s) % 4, col, layer) for s in range(1, 4)]
+    far = (4 * (1 - high) + x, col, layer)
     barrier = pltpu.get_barrier_semaphore()
-    peers = [((row + s) % 8, col, layer) for s in range(1, 8)]
-    for peer in peers:
+    for peer in near + [far]:
         pl.semaphore_signal(barrier, inc=1, device_id=peer, device_id_type=MESH)
-    slots[row] = sums_ref[...]
-    pl.semaphore_wait(barrier, 7)
-    copies = [
-        pltpu.make_async_remote_copy(
-            src_ref=slots.at[row],
-            dst_ref=slots.at[row],
-            send_sem=send_sems.at[s],
-            recv_sem=recv_sems.at[s],
+    slots[x] = sums_ref[...]
+    pl.semaphore_wait(barrier, 4)
+
+    def swap(k, src, dst, peer):
+        return pltpu.make_async_remote_copy(
+            src_ref=slots.at[src],
+            dst_ref=slots.at[dst],
+            send_sem=send_sems.at[k],
+            recv_sem=recv_sems.at[k],
             device_id=peer,
             device_id_type=MESH,
         )
-        for s, peer in enumerate(peers)
-    ]
+
+    copies = [swap(k, x, x, peer) for k, peer in enumerate(near)]
     for copy in copies:
         copy.start()
     for copy in copies:
         copy.wait()
-    total = slots[0]
-    for q in range(1, 8):
-        total = total + slots[q]
-    out_ref[...] = jnp.sum(total, axis=0, keepdims=True)
+    slots[4] = (slots[0] + slots[1]) + (slots[2] + slots[3])
+    copy = swap(3, 4, 5, far)
+    copy.start()
+    copy.wait()
+    out_ref[...] = slots[4] + slots[5]
 
 
 def reduce_totals(sums):
     return pl.pallas_call(
         totals_kernel,
-        out_shape=jax.ShapeDtypeStruct((1, sums.shape[1]), jnp.float32),
+        out_shape=pltpu.VMEM(sums.shape, jnp.float32),
         in_specs=[pl.BlockSpec(memory_space=pltpu.VMEM)],
         out_specs=pl.BlockSpec(memory_space=pltpu.VMEM),
         scratch_shapes=[
-            pltpu.VMEM((8,) + sums.shape, jnp.float32),
-            pltpu.SemaphoreType.DMA((7,)),
-            pltpu.SemaphoreType.DMA((7,)),
+            pltpu.VMEM((6,) + sums.shape, jnp.float32),
+            pltpu.SemaphoreType.DMA((4,)),
+            pltpu.SemaphoreType.DMA((4,)),
         ],
         compiler_params=pltpu.CompilerParams(
             collective_id=1, has_side_effects=True, vmem_limit_bytes=4 * MIB

time: 69 us -> 65.8 us (0.954); the launches traced: 68.6 us -> 64.7 us
  Pallas kernels: 68.6 us -> 64.6 us
    pallas_call x1, Pallas kernels: 46.6 us -> 44.2 us  [gather(): pl.pallas_call(gather_kernel, out_shape=[pltpu.VMEM((16, SHARE, BLK), sha...]
    pallas_call x1, Pallas kernels: 7.77 us -> 5.42 us  [product(): pl.pallas_call(product_kernel, out_shape=[pltpu.VMEM((out_rows, lanes), j...]
    pallas_call x1, Pallas kernels: 9.82 us -> 10.6 us  [reduce_totals(): pl.pallas_call(totals_kernel, out_shape=pltpu.VMEM(sums.shape, jnp.float3...]
where the time goes in v4:
time: 65.8 us; the launch traced here: 64.7 us
  Pallas kernels  64.6 us (98%)
    pallas_call x1, Pallas kernels, gather(): pl.pallas_call(gather_kernel, out_shape=[pltpu.VMEM((16, SHARE, BLK), sha...  44.2 us
    pallas_call x1, Pallas kernels, reduce_totals(): pl.pallas_call(totals_kernel, out_shape=pltpu.VMEM(sums.shape, jnp.float3...  10.6 us
    pallas_call x1, Pallas kernels, product(): pl.pallas_call(product_kernel, out_shape=[pltpu.VMEM((out_rows, lanes), j...  5.42 us
    pallas_call x1, Pallas kernels, scale(): pl.pallas_call(functools.partial(scale_kernel, scaling), out_shape=jax.Sh...  2.28 us
    pallas_call x1, Pallas kernels, pack(): pl.pallas_call(pack_kernel, out_shape=pltpu.VMEM((SHARE, BLK), similarity...  2.03 us

profile of v4, /device:TPU:0, one launch (start us, length us, event | category | flops | bytes accessed | tf_op | source)
XLA Modules:
  0.0 64.7 jit_solution(907070922787772624)
XLA Ops:
  0.0 2.0 %pack.1.share_ref = bf16[2336,128]{1,0:T(8,128)(2,1)S(1)} custom-call(s32[6,12]{1,0:T(8,128)} %bitcast.1, bf16[1536,768]{1,0:T(8,128)(2,1)} %x_ref.1), custom_call_target="tpu_custom_call" | custom-call | tf_op jit(solution)/shard_map/pack/pallas_call | solution.py:62
  2.0 44.2 %gather.1 = (bf16[16,2336,128]{2,1,0:T(8,128)(2,1)S(1)}, bf16[8,2336,128]{2,1,0:T(8,128)(2,1)S(1)}) custom-call(bf16[2336,128]{1,0:T(8,128)(2,1)S(1)} %pack.1.share_ref), custom_call_target="tpu_custom_call" | custom-call | tf_op jit(solution)/shard_map/gather/pallas_call | solution.py:297
  46.3 5.4 %product.1 = (f32[1536,768]{1,0:T(8,128)S(1)}, f32[1,768]{1,0:T(1,128)S(1)}) custom-call(bf16[16,2336,128]{2,1,0:T(8,128)(2,1)S(1)} %get-tuple-element.9.r_ref, bf16[8,2336,128]{2,1,0:T(8,128)(2,1)S(1)} %get-tuple-element.10.c_ref), custom_call_target="tpu_custom_call" | custom-call | tf_op jit(solution)/shard_map/product/pallas_call | solution.py:425
  51.7 10.6 %totals.1.total_ref = f32[1,768]{1,0:T(1,128)S(1)} custom-call(f32[1,768]{1,0:T(1,128)S(1)} %get-tuple-element.12.sums_ref), custom_call_target="tpu_custom_call" | custom-call | tf_op jit(solution)/shard_map/totals/pallas_call | solution.py:477
  62.4 2.3 %scale.1 = f32[1536,768]{1,0:T(8,128)} custom-call(f32[1536,768]{1,0:T(8,128)S(1)} %get-tuple-element.11.value_ref, f32[1,768]{1,0:T(1,128)S(1)} %totals.1.total_ref), custom_call_target="tpu_custom_call" | custom-call | tf_op jit(solution)/shard_map/scale/pallas_call | solution.py:513

commit v5 on v4

--- a/solution.py
+++ b/solution.py
@@ -16,61 +16,52 @@
 MESH = pl.DeviceIdType.MESH
 
 
-def pack_kernel(mask_ref, x_ref, share_ref, sems):
+def pack_share(mask_ref, x_ref, x_v, share, place_v, place_s, sems):
     cols, rows = mask_ref.shape
+    strips = x_v.reshape(cols * rows * BLK, BLK)
+    loads = [
+        pltpu.make_async_copy(
+            x_ref.at[:, pl.ds(j * BLK, BLK)],
+            strips.at[pl.ds(j * rows * BLK, rows * BLK)],
+            sems.at[j],
+        )
+        for j in range(cols)
+    ]
+    for load in loads:
+        load.start()
     sub = lax.broadcasted_iota(jnp.int32, (HEAD, BLK), 0)
     lane = lax.broadcasted_iota(jnp.int32, (HEAD, BLK), 1)
     lane_row = (lane * 43) >> 8
     lane_col = lane - lane_row * cols
+    lane8 = lane[:8]
 
     def one_row(i, carry):
-        count, head = carry
+        count, head, place = carry
         below = 8 + jnp.where(i < cols, i, i - cols + 8)
         for j in range(cols):
             here = mask_ref[j, i]
-
-            @pl.when(here > 0)
-            def _():
-                pltpu.make_async_copy(
-                    x_ref.at[pl.ds(i * BLK, BLK), pl.ds(j * BLK, BLK)],
-                    share_ref.at[pl.ds(pl.multiple_of(HEAD + count * BLK, HEAD), BLK)],
-                    sems.at[count],
-                ).start()
-
             cell = ((sub == j) & (lane_row == i)) | ((sub == below) & (lane_col == j))
-            head = jnp.where(cell & (here > 0), count + 1, head)
+            head = head + jnp.where(cell, here * (count + 1), 0)
+            place = place + jnp.where(lane8 == count, here * (j * rows + i), 0)
             count = count + here
-        return count, head
-
-    count, head = lax.fori_loop(
-        0, rows, one_row, (jnp.int32(0), jnp.zeros((HEAD, BLK), jnp.int32))
+        return count, head, place
+
+    _, head, place = lax.fori_loop(
+        0,
+        rows,
+        one_row,
+        (jnp.int32(0), jnp.zeros((HEAD, BLK), jnp.int32), jnp.zeros((8, BLK), jnp.int32)),
     )
+    place_v[...] = place
+    move = pltpu.make_async_copy(place_v, place_s, sems.at[cols])
+    move.start()
     head = jnp.where(lane < rows * cols, head, 0)
-    share_ref[pl.ds(0, HEAD), :] = head.astype(jnp.float32).astype(share_ref.dtype)
+    share[pl.ds(0, HEAD), :] = head.astype(jnp.float32).astype(share.dtype)
+    move.wait()
+    for load in loads:
+        load.wait()
     for s in range(MAXNZ):
-
-        @pl.when(s < count)
-        def _():
-            pltpu.make_async_copy(
-                x_ref.at[pl.ds(0, BLK), pl.ds(0, BLK)],
-                share_ref.at[pl.ds(HEAD + s * BLK, BLK)],
-                sems.at[s],
-            ).wait()
-
-
-def pack(block_mask, similarity):
-    return pl.pallas_call(
-        pack_kernel,
-        out_shape=pltpu.VMEM((SHARE, BLK), similarity.dtype),
-        in_specs=[
-            pl.BlockSpec(memory_space=pltpu.SMEM),
-            pl.BlockSpec(memory_space=pl.ANY),
-        ],
-        out_specs=pl.BlockSpec(memory_space=pltpu.VMEM),
-        scratch_shapes=[pltpu.SemaphoreType.DMA((MAXNZ,))],
-        compiler_params=pltpu.CompilerParams(vmem_limit_bytes=56 * MIB),
-        name="pack",
-    )(block_mask.T, similarity)
+        share[pl.ds(HEAD + s * BLK, BLK), :] = x_v[place_s[0, s]]
 
 
 LAST = 5
@@ -83,7 +74,19 @@
 
 
 def gather_kernel(
-    share_ref, rows_ref, cols_ref, relay, send_sems, recv_sems, own_sems
+    mask_ref,
+    x_ref,
+    rows_ref,
+    cols_ref,
+    x_v,
+    share_ref,
+    relay,
+    place_v,
+    place_s,
+    send_sems,
+    recv_sems,
+    own_sems,
+    pack_sems,
 ):
     row, col, layer = (lax.axis_index(a) for a in ("row", "col", "layer"))
     high, x = row // 4, row % 4
@@ -106,6 +109,7 @@
     barrier = pltpu.get_barrier_semaphore()
     for peer in (zp, zm, xp, xm, lo, hi, sib):
         pl.semaphore_signal(barrier, inc=1, device_id=peer, device_id_type=MESH)
+    pack_share(mask_ref, x_ref, x_v, share_ref, place_v, place_s, pack_sems)
     pl.semaphore_wait(barrier, 7)
 
     mine = 2 * col + layer
@@ -293,26 +297,36 @@
 COPIES = 53
 
 
-def gather(share):
+def gather(block_mask, similarity):
+    dtype = similarity.dtype
+    cells = block_mask.size
     return pl.pallas_call(
         gather_kernel,
         out_shape=[
-            pltpu.VMEM((16, SHARE, BLK), share.dtype),
-            pltpu.VMEM((8, SHARE, BLK), share.dtype),
-        ],
-        in_specs=[pl.BlockSpec(memory_space=pltpu.VMEM)],
+            pltpu.VMEM((16, SHARE, BLK), dtype),
+            pltpu.VMEM((8, SHARE, BLK), dtype),
+        ],
+        in_specs=[
+            pl.BlockSpec(memory_space=pltpu.SMEM),
+            pl.BlockSpec(memory_space=pl.ANY),
+        ],
         out_specs=[pl.BlockSpec(memory_space=pltpu.VMEM)] * 2,
         scratch_shapes=[
-            pltpu.VMEM((3, LAST * BLK, BLK), share.dtype),
+            pltpu.VMEM((cells, BLK, BLK), dtype),
+            pltpu.VMEM((SHARE, BLK), dtype),
+            pltpu.VMEM((3, LAST * BLK, BLK), dtype),
+            pltpu.VMEM((8, BLK), jnp.int32),
+            pltpu.SMEM((8, BLK), jnp.int32),
             pltpu.SemaphoreType.DMA((COPIES,)),
             pltpu.SemaphoreType.DMA((COPIES,)),
             pltpu.SemaphoreType.DMA((2,)),
+            pltpu.SemaphoreType.DMA((7,)),
         ],
         compiler_params=pltpu.CompilerParams(
-            collective_id=0, has_side_effects=True, vmem_limit_bytes=32 * MIB
+            collective_id=0, has_side_effects=True, vmem_limit_bytes=44 * MIB
         ),
         name="gather",
-    )(share)
+    )(block_mask.T, similarity)
 
 
 GROUP = 4
@@ -525,7 +539,7 @@
 
 
 def body(similarity, block_mask):
-    rows, cols = gather(pack(block_mask, similarity))
+    rows, cols = gather(block_mask, similarity)
     value, sums = product(rows, cols, *similarity.shape)
     total = reduce_totals(sums)
     scaling = similarity.shape[0] * lax.axis_size("row")

time: 65.8 us -> 64.7 us (0.983); the launches traced: 64.7 us -> 64.5 us
    pallas_call x2 -> x1, Pallas kernels: 46.3 us -> 45 us  [gather(): pl.pallas_call(gather_kernel, out_shape=[pltpu.VMEM((16, SHARE, BLK), dty...]
where the time goes in v5:
time: 64.7 us; the launch traced here: 64.5 us
  Pallas kernels  64.5 us (100%)
    pallas_call x1, Pallas kernels, gather(): pl.pallas_call(gather_kernel, out_shape=[pltpu.VMEM((16, SHARE, BLK), dty...  45 us
    pallas_call x1, Pallas kernels, reduce_totals(): pl.pallas_call(totals_kernel, out_shape=pltpu.VMEM(sums.shape, jnp.float3...  11.2 us
    pallas_call x1, Pallas kernels, product(): pl.pallas_call(product_kernel, out_shape=[pltpu.VMEM((out_rows, lanes), j...  6.01 us
    pallas_call x1, Pallas kernels, scale(): pl.pallas_call(functools.partial(scale_kernel, scaling), out_shape=jax.Sh...  2.28 us

profile of v5, /device:TPU:0, one launch (start us, length us, event | category | flops | bytes accessed | tf_op | source)
XLA Modules:
  0.0 64.5 jit_solution(3488861823987511145)
XLA Ops:
  0.0 45.0 %gather.1 = (bf16[16,2336,128]{2,1,0:T(8,128)(2,1)S(1)}, bf16[8,2336,128]{2,1,0:T(8,128)(2,1)S(1)}) custom-call(s32[6,12]{1,0:T(8,128)} %bitcast.1, bf16[1536,768]{1,0:T(8,128)(2,1)} %x_ref.1), custom_call_target="tpu_custom_call" | custom-call | tf_op jit(solution)/shard_map/gather/pallas_call | solution.py:303
  45.0 6.0 %product.1 = (f32[1536,768]{1,0:T(8,128)S(1)}, f32[1,768]{1,0:T(1,128)S(1)}) custom-call(bf16[16,2336,128]{2,1,0:T(8,128)(2,1)S(1)} %get-tuple-element.9.r_ref, bf16[8,2336,128]{2,1,0:T(8,128)(2,1)S(1)} %get-tuple-element.10.c_ref), custom_call_target="tpu_custom_call" | custom-call | tf_op jit(solution)/shard_map/product/pallas_call | solution.py:439
  51.0 11.2 %totals.1.total_ref = f32[1,768]{1,0:T(1,128)S(1)} custom-call(f32[1,768]{1,0:T(1,128)S(1)} %get-tuple-element.12.sums_ref), custom_call_target="tpu_custom_call" | custom-call | tf_op jit(solution)/shard_map/totals/pallas_call | solution.py:491
  62.2 2.3 %scale.1 = f32[1536,768]{1,0:T(8,128)} custom-call(f32[1536,768]{1,0:T(8,128)S(1)} %get-tuple-element.11.value_ref, f32[1,768]{1,0:T(1,128)S(1)} %totals.1.total_ref), custom_call_target="tpu_custom_call" | custom-call | tf_op jit(solution)/shard_map/scale/pallas_call | solution.py:527

commit v6 on v5

--- a/solution.py
+++ b/solution.py
@@ -11,7 +11,11 @@
 MAXNZ = 18
 HEAD = 32
 HALF = MAXNZ // 2
-SHARE = HEAD + MAXNZ * BLK
+SLOTS = MAXNZ + 1
+SHARE = SLOTS * BLK
+TOP = BLK - HEAD
+GROUP = 4
+DEPTH = 16
 MIB = 1 << 20
 MESH = pl.DeviceIdType.MESH
 
@@ -35,33 +39,75 @@
     lane_col = lane - lane_row * cols
     lane8 = lane[:8]
 
-    def one_row(i, carry):
-        count, head, place = carry
+    def find(i, carry):
+        count, place = carry
+        for j in range(cols):
+            here = mask_ref[j, i]
+            place = place + jnp.where(lane8 == count, here * (j * rows + i), 0)
+            count = count + here
+        return count, place
+
+    zero = jnp.int32(0)
+    _, place = lax.fori_loop(0, rows, find, (zero, jnp.zeros((8, BLK), jnp.int32)), unroll=3)
+    place_v[...] = place
+    move = pltpu.make_async_copy(place_v, place_s, sems.at[cols])
+    move.start()
+
+    def mark(i, carry):
+        count, head = carry
         below = 8 + jnp.where(i < cols, i, i - cols + 8)
         for j in range(cols):
             here = mask_ref[j, i]
             cell = ((sub == j) & (lane_row == i)) | ((sub == below) & (lane_col == j))
             head = head + jnp.where(cell, here * (count + 1), 0)
-            place = place + jnp.where(lane8 == count, here * (j * rows + i), 0)
             count = count + here
-        return count, head, place
-
-    _, head, place = lax.fori_loop(
-        0,
-        rows,
-        one_row,
-        (jnp.int32(0), jnp.zeros((HEAD, BLK), jnp.int32), jnp.zeros((8, BLK), jnp.int32)),
-    )
-    place_v[...] = place
-    move = pltpu.make_async_copy(place_v, place_s, sems.at[cols])
-    move.start()
+        return count, head
+
+    _, head = lax.fori_loop(0, rows, mark, (zero, jnp.zeros((HEAD, BLK), jnp.int32)))
     head = jnp.where(lane < rows * cols, head, 0)
-    share[pl.ds(0, HEAD), :] = head.astype(jnp.float32).astype(share.dtype)
+    share[pl.ds(TOP, HEAD), :] = head.astype(jnp.float32).astype(share.dtype)
     move.wait()
     for load in loads:
         load.wait()
     for s in range(MAXNZ):
-        share[pl.ds(HEAD + s * BLK, BLK), :] = x_v[place_s[0, s]]
+        share[pl.ds((s + 1) * BLK, BLK), :] = x_v[place_s[0, s]]
+
+
+def pair_lists(rows_ref, cols_ref):
+    hr, hc = [], []
+    for q in range(16):
+        hr.append(rows_ref[q, pl.ds(TOP, HEAD), :].astype(jnp.float32)[0:8])
+    for q in range(8):
+        top = cols_ref[q, pl.ds(TOP, HEAD), :].astype(jnp.float32)
+        hc += [top[8:16], top[16:24]]
+    hr, hc = jnp.concatenate(hr, 0), jnp.concatenate(hc, 0)
+    both = jnp.where((hr > 0) & (hc > 0), 1.0, 0.0)
+    line = lax.broadcasted_iota(jnp.int32, (BLK, BLK), 0)
+    before = line > lax.broadcasted_iota(jnp.int32, (BLK, BLK), 1)
+    rank = jnp.dot(
+        jnp.where(before, 1.0, 0.0).astype(jnp.bfloat16),
+        both.astype(jnp.bfloat16),
+        preferred_element_type=jnp.float32,
+    )
+    rank = jnp.where(both > 0, rank, -1.0).astype(jnp.int32)
+    place_r = (line >> 3) * SLOTS + hr.astype(jnp.int32)
+    place_c = (line >> 4) * SLOTS + hc.astype(jnp.int32)
+    count = jnp.sum(both, axis=0, keepdims=True).astype(jnp.int32)
+    return rank, place_r, place_c, count
+
+
+def write_lists(table_v, lists, done):
+    rank, place_r, place_c, count = lists
+    for p in range(DEPTH):
+        at = rank == done + p
+        some = count > done + p
+        first = jnp.sum(jnp.where(at, place_r, 0), axis=0, keepdims=True)
+        second = jnp.sum(jnp.where(at, place_c, 0), axis=0, keepdims=True)
+        table_v[pl.ds(p, 1), :] = jnp.where(some, first, 16 * SLOTS)
+        table_v[pl.ds(DEPTH + p, 1), :] = jnp.where(some, second, 1)
+    most = jnp.max(count, axis=1, keepdims=True)
+    table_v[pl.ds(2 * DEPTH, 1), :] = count - done
+    table_v[pl.ds(2 * DEPTH + 1, 1), :] = jnp.broadcast_to(most, count.shape)
 
 
 LAST = 5
@@ -69,8 +115,8 @@
 
 
 def span(first, last):
-    low = HEAD + first * BLK if first else 0
-    return pl.ds(low, HEAD + last * BLK - low)
+    low = (first + 1) * BLK if first else TOP
+    return pl.ds(low, (last + 1) * BLK - low)
 
 
 def gather_kernel(
@@ -78,6 +124,7 @@
     x_ref,
     rows_ref,
     cols_ref,
+    table_ref,
     x_v,
     share_ref,
     relay,
@@ -87,6 +134,7 @@
     recv_sems,
     own_sems,
     pack_sems,
+    table_v,
 ):
     row, col, layer = (lax.axis_index(a) for a in ("row", "col", "layer"))
     high, x = row // 4, row % 4
@@ -112,14 +160,14 @@
     pack_share(mask_ref, x_ref, x_v, share_ref, place_v, place_s, pack_sems)
     pl.semaphore_wait(barrier, 7)
 
+    ALL = span(0, MAXNZ)
     mine = 2 * col + layer
     keep = [
-        pltpu.make_async_copy(share_ref, rows_ref.at[mine], own_sems.at[0]),
-        pltpu.make_async_copy(share_ref, cols_ref.at[row], own_sems.at[1]),
+        pltpu.make_async_copy(share_ref.at[ALL], rows_ref.at[mine].at[ALL], own_sems.at[0]),
+        pltpu.make_async_copy(share_ref.at[ALL], cols_ref.at[row].at[ALL], own_sems.at[1]),
     ]
 
     EARLY = MAXNZ - LAST
-    ALL = span(0, MAXNZ)
     H1, H2 = span(0, HALF), span(HALF, MAXNZ)
     U1, U2, L = span(0, SPLIT), span(SPLIT, EARLY), span(EARLY, MAXNZ)
     V1, V2, V3, V4 = span(0, 4), span(4, SPLIT), span(SPLIT, 10), span(10, EARLY)
@@ -188,6 +236,7 @@
     sb0 = send(share_ref, own_r, ALL, sib)
     for copy in keep:
         copy.start()
+    rows_ref[16, pl.ds(0, BLK), :] = jnp.zeros((BLK, BLK), rows_ref.dtype)
 
     arrived(lo1, y_r, U1, lo)
     hi1 = send(y_r, own_c, U1, hi)
@@ -264,17 +313,12 @@
     arrived(gzq, yy_r, V2, zm)
     sb11 = send(yy_r, yy_r, V2, sib)
 
-    arrived(hi3, y_c, L, hi)
+    for copy in keep:
+        copy.wait()
     arrived(xm1, xp_c, H1, xp)
     arrived(fxp, xx_c, H1, xm)
-    arrived(yxp2, ym_c, U2, xm)
     arrived(yxm1, yp_c, U1, xp)
-    arrived(uxp, yp_c, L, hi)
-    arrived(uxm, ym_c, L, hi)
-    arrived(uxx, yy_c, L, hi)
     arrived(gxp, yy_c, U1, xm)
-    arrived(gxm, yy_c, U2, xp)
-
     arrived(sb0, rsib(col), ALL, sib)
     arrived(sb1, rsib(mate), ALL, sib)
     arrived(sb2, rsib(along_z(3)), ALL, sib)
@@ -282,16 +326,25 @@
     arrived(sb4, rsib(along_z(2)), ALL, sib)
     arrived(sb5, rsib(other(along_z(1))), ALL, sib)
     arrived(sb6, rsib(other(along_z(3))), ALL, sib)
+    arrived(sb8, rsib(other(along_z(2))), V1, sib)
+    write_lists(table_v, pair_lists(rows_ref, cols_ref), 0)
+    hand = pltpu.make_async_copy(table_v, table_ref, own_sems.at[2])
+    hand.start()
+
+    arrived(hi3, y_c, L, hi)
+    arrived(yxp2, ym_c, U2, xm)
+    arrived(uxp, yp_c, L, hi)
+    arrived(uxm, ym_c, L, hi)
+    arrived(uxx, yy_c, L, hi)
+    arrived(gxm, yy_c, U2, xp)
     arrived(sb7, rsib(other(along_z(2))), L, sib)
-    arrived(sb8, rsib(other(along_z(2))), V1, sib)
     arrived(sb9, rsib(other(along_z(2))), V3, sib)
     arrived(sb10, rsib(other(along_z(2))), V4, sib)
     arrived(sb11, rsib(other(along_z(2))), V2, sib)
     assert waited == set(range(len(started))) and len(started) == COPIES
     for copy in started:
         copy.wait_send()
-    for copy in keep:
-        copy.wait()
+    hand.wait()
 
 
 COPIES = 53
@@ -303,14 +356,19 @@
     return pl.pallas_call(
         gather_kernel,
         out_shape=[
-            pltpu.VMEM((16, SHARE, BLK), dtype),
+            pltpu.VMEM((17, SHARE, BLK), dtype),
             pltpu.VMEM((8, SHARE, BLK), dtype),
+            pltpu.SMEM((2 * DEPTH + 8, BLK), jnp.int32),
         ],
         in_specs=[
             pl.BlockSpec(memory_space=pltpu.SMEM),
             pl.BlockSpec(memory_space=pl.ANY),
         ],
-        out_specs=[pl.BlockSpec(memory_space=pltpu.VMEM)] * 2,
+        out_specs=[
+            pl.BlockSpec(memory_space=pltpu.VMEM),
+            pl.BlockSpec(memory_space=pltpu.VMEM),
+            pl.BlockSpec(memory_space=pltpu.SMEM),
+        ],
         scratch_shapes=[
             pltpu.VMEM((cells, BLK, BLK), dtype),
             pltpu.VMEM((SHARE, BLK), dtype),
@@ -319,8 +377,9 @@
             pltpu.SMEM((8, BLK), jnp.int32),
             pltpu.SemaphoreType.DMA((COPIES,)),
             pltpu.SemaphoreType.DMA((COPIES,)),
-            pltpu.SemaphoreType.DMA((2,)),
+            pltpu.SemaphoreType.DMA((3,)),
             pltpu.SemaphoreType.DMA((7,)),
+            pltpu.VMEM((2 * DEPTH + 8, BLK), jnp.int32),
         ],
         compiler_params=pltpu.CompilerParams(
             collective_id=0, has_side_effects=True, vmem_limit_bytes=44 * MIB
@@ -329,132 +388,91 @@
     )(block_mask.T, similarity)
 
 
-GROUP = 4
-DEPTH = 16
-
-
-def product_kernel(r_ref, c_ref, out_ref, sums_ref, table_v, table_s, sem):
-    tiles, lanes = out_ref.shape[0] // BLK, out_ref.shape[1]
-    wide = lanes // BLK
-    col = lax.axis_index("col")
-
-    hr, hc = [], []
-    for q in range(16):
-        hr.append(r_ref[q, pl.ds(0, HEAD), :].astype(jnp.float32)[0:8])
-    for q in range(8):
-        top = c_ref[q, pl.ds(0, HEAD), :].astype(jnp.float32)
-        hc += [top[8:16], top[16:24]]
-    hr, hc = jnp.concatenate(hr, 0), jnp.concatenate(hc, 0)
-    both = (hr > 0) & (hc > 0)
-    line = lax.broadcasted_iota(jnp.int32, (BLK, BLK), 0)
-    rank = jnp.dot(
-        (line > lax.broadcasted_iota(jnp.int32, (BLK, BLK), 1)).astype(jnp.bfloat16),
-        both.astype(jnp.float32).astype(jnp.bfloat16),
-        preferred_element_type=jnp.float32,
+def group_product(r_ref, c_ref, table, cell, g):
+    return sum(
+        jnp.dot(
+            r_ref[table[p, cell]],
+            c_ref[table[DEPTH + p, cell]],
+            preferred_element_type=jnp.float32,
+        )
+        for p in [g * GROUP + t for t in range(GROUP)]
     )
-    rank = jnp.where(both, rank, -1.0).astype(jnp.int32)
-    place_r = (line >> 3) * SHARE + (HEAD - BLK) + hr.astype(jnp.int32) * BLK
-    place_c = (line >> 4) * SHARE + (HEAD - BLK) + hc.astype(jnp.int32) * BLK
-    count = jnp.sum(both.astype(jnp.int32), axis=0, keepdims=True)
-    most = jnp.max(count)
-    idle_c = col * SHARE + HEAD
-
-    def fill(done):
-        for p in range(DEPTH):
-            at = rank == done + p
-            some = count > done + p
-            first = jnp.sum(jnp.where(at, place_r, 0), axis=0, keepdims=True)
-            second = jnp.sum(jnp.where(at, place_c, 0), axis=0, keepdims=True)
-            table_v[pl.ds(p, 1), :] = jnp.where(some, first, HEAD)
-            table_v[pl.ds(DEPTH + p, 1), :] = jnp.where(some, second, idle_c)
-        table_v[pl.ds(2 * DEPTH, 1), :] = jnp.clip(count - done, 0, DEPTH)
+
+
+def as_blocks(ref):
+    return ref.reshape(ref.shape[0] * SLOTS, BLK, BLK)
+
+
+def later_kernel(rows_ref, cols_ref, table_ref, extra_ref, table_v, table_s, sem):
+    r_ref, c_ref = as_blocks(rows_ref), as_blocks(cols_ref)
+    tiles, wide = extra_ref.shape[0] // BLK, extra_ref.shape[1] // BLK
+
+    def here(i, j):
+        return pl.ds(pl.multiple_of(i * BLK, BLK), BLK), pl.ds(j * BLK, BLK)
+
+    def groups(table, cell):
+        return (jnp.minimum(table[2 * DEPTH, cell], DEPTH) + GROUP - 1) // GROUP
+
+    def add(table, i, j, first):
+        cell = i * wide + j
+
+        @pl.loop(first, groups(table, cell))
+        def _(g):
+            extra_ref[here(i, j)] += group_product(r_ref, c_ref, table, cell, g)
+
+    @pl.loop(0, tiles)
+    def _(i):
+        top = table_ref[2 * DEPTH, i * wide]
+        for j in range(1, wide):
+            top = jnp.maximum(top, table_ref[2 * DEPTH, i * wide + j])
+
+        @pl.when(top > GROUP)
+        def _():
+            for j in range(wide):
+                cell = i * wide + j
+
+                @pl.when(table_ref[2 * DEPTH, cell] > GROUP)
+                def _():
+                    extra_ref[here(i, j)] = group_product(r_ref, c_ref, table_ref, cell, 1)
+                    add(table_ref, i, j, 2)
+
+    most = table_ref[2 * DEPTH + 1, 0]
+
+    @pl.loop(1, (most + DEPTH - 1) // DEPTH)
+    def _(d):
+        write_lists(table_v, pair_lists(rows_ref, cols_ref), d * DEPTH)
         copy = pltpu.make_async_copy(table_v, table_s, sem)
         copy.start()
         copy.wait()
 
-    def part(i, j, g):
-        cell = i * wide + j
-        left, right = [], []
-        have = table_s[2 * DEPTH, cell]
-        for t in range(GROUP):
-            p = g * GROUP + t
-            a = r_ref[pl.ds(pl.multiple_of(table_s[p, cell], HEAD), BLK), :]
-            left.append(jnp.where(p < have, a, jnp.zeros_like(a)))
-            right.append(c_ref[pl.ds(pl.multiple_of(table_s[DEPTH + p, cell], HEAD), BLK), :])
-        return sum(
-            jnp.dot(a, b, preferred_element_type=jnp.float32) for a, b in zip(left, right)
-        )
-
-    def more(i, j, first):
-        here = pl.ds(pl.multiple_of(i * BLK, BLK), BLK)
-
-        @pl.loop(first, (table_s[2 * DEPTH, i * wide + j] + GROUP - 1) // GROUP)
-        def _(g):
-            out_ref[here, pl.ds(j * BLK, BLK)] += part(i, j, g)
-
-    fill(0)
-    r_ref = r_ref.reshape(16 * SHARE, BLK)
-    c_ref = c_ref.reshape(8 * SHARE, BLK)
-
-    @pl.loop(0, tiles, unroll=3)
-    def _(i):
-        here = pl.ds(pl.multiple_of(i * BLK, BLK), BLK)
-        for j in range(wide):
-            out_ref[here, pl.ds(j * BLK, BLK)] = part(i, j, 0)
-
-    @pl.loop(0, tiles)
-    def _(i):
-        top = table_s[2 * DEPTH, i * wide]
-        for j in range(1, wide):
-            top = jnp.maximum(top, table_s[2 * DEPTH, i * wide + j])
-
-        @pl.when(top > GROUP)
-        def _():
-            for j in range(wide):
-                more(i, j, 1)
-
-    @pl.loop(1, (most + DEPTH - 1) // DEPTH)
-    def _(d):
-        fill(d * DEPTH)
-
         @pl.loop(0, tiles)
         def _(i):
             for j in range(wide):
-                more(i, j, 0)
-
-    def square(t, total):
-        here = pl.ds(pl.multiple_of(t * 64, 64), 64)
-        value = out_ref[here, :]
-        value = value * value
-        out_ref[here, :] = value
-        return total + jnp.sum(value.reshape(8, 8, lanes), axis=0)
-
-    total = lax.fori_loop(
-        0, tiles * BLK // 64, square, jnp.zeros((8, lanes), jnp.float32)
-    )
-    sums_ref[...] = jnp.sum(total, axis=0, keepdims=True)
-
-
-def product(rows, cols, out_rows, lanes):
+                add(table_s, i, j, 0)
+
+
+VMEM, SMEM = pl.BlockSpec(memory_space=pltpu.VMEM), pl.BlockSpec(memory_space=pltpu.SMEM)
+
+
+def later(rows, cols, table, shape):
     return pl.pallas_call(
-        product_kernel,
-        out_shape=[
-            pltpu.VMEM((out_rows, lanes), jnp.float32),
-            pltpu.VMEM((1, lanes), jnp.float32),
-        ],
-        in_specs=[pl.BlockSpec(memory_space=pltpu.VMEM)] * 2,
-        out_specs=[pl.BlockSpec(memory_space=pltpu.VMEM)] * 2,
+        later_kernel,
+        out_shape=pltpu.VMEM(shape, jnp.float32),
+        in_specs=[VMEM, VMEM, SMEM],
+        out_specs=VMEM,
         scratch_shapes=[
-            pltpu.VMEM((2 * DEPTH + 8, BLK), jnp.int32),
-            pltpu.SMEM((2 * DEPTH + 8, BLK), jnp.int32),
+            pltpu.VMEM(table.shape, jnp.int32),
+            pltpu.SMEM(table.shape, jnp.int32),
             pltpu.SemaphoreType.DMA(()),
         ],
         compiler_params=pltpu.CompilerParams(vmem_limit_bytes=8 * MIB),
-        name="product",
-    )(rows, cols)
-
-
-def totals_kernel(sums_ref, out_ref, slots, send_sems, recv_sems):
+        name="later",
+    )(rows, cols, table)
+
+
+def product_kernel(
+    rows_ref, cols_ref, table_ref, extra_ref, out_ref, total_ref, slots, send_sems, recv_sems
+):
     row, col, layer = (lax.axis_index(a) for a in ("row", "col", "layer"))
     high, x = row // 4, row % 4
     near = [(4 * high + (x + s) % 4, col, layer) for s in range(1, 4)]
@@ -462,7 +480,26 @@
     barrier = pltpu.get_barrier_semaphore()
     for peer in near + [far]:
         pl.semaphore_signal(barrier, inc=1, device_id=peer, device_id_type=MESH)
-    slots[x] = sums_ref[...]
+
+    r_ref, c_ref = as_blocks(rows_ref), as_blocks(cols_ref)
+    tiles, wide = out_ref.shape[0] // BLK, out_ref.shape[1] // BLK
+
+    def one_row(i, sums):
+        lines = pl.ds(pl.multiple_of(i * BLK, BLK), BLK)
+        out = []
+        for j in range(wide):
+            cell = i * wide + j
+            value = group_product(r_ref, c_ref, table_ref, cell, 0)
+            has_more = jnp.full((BLK, BLK), table_ref[2 * DEPTH, cell], jnp.int32) > GROUP
+            value = value + jnp.where(has_more, extra_ref[lines, pl.ds(j * BLK, BLK)], 0.0)
+            value = value * value
+            out_ref[lines, pl.ds(j * BLK, BLK)] = value
+            out.append(sums[j] + jnp.sum(value.reshape(BLK // 8, 8, BLK), axis=0))
+        return tuple(out)
+
+    sums = tuple(jnp.zeros((8, BLK), jnp.float32) for _ in range(wide))
+    sums = lax.fori_loop(0, tiles, one_row, sums, unroll=3)
+    slots[x] = jnp.concatenate([jnp.sum(v, axis=0, keepdims=True) for v in sums], 1)
     pl.semaphore_wait(barrier, 4)
 
     def swap(k, src, dst, peer):
@@ -484,25 +521,26 @@
     copy = swap(3, 4, 5, far)
     copy.start()
     copy.wait()
-    out_ref[...] = slots[4] + slots[5]
-
-
-def reduce_totals(sums):
+    total_ref[...] = slots[4] + slots[5]
+
+
+def product(rows, cols, table, extra):
+    lanes = extra.shape[1]
     return pl.pallas_call(
-        totals_kernel,
-        out_shape=pltpu.VMEM(sums.shape, jnp.float32),
-        in_specs=[pl.BlockSpec(memory_space=pltpu.VMEM)],
-        out_specs=pl.BlockSpec(memory_space=pltpu.VMEM),
+        product_kernel,
+        out_shape=[pltpu.VMEM(extra.shape, jnp.float32), pltpu.VMEM((1, lanes), jnp.float32)],
+        in_specs=[VMEM, VMEM, SMEM, VMEM],
+        out_specs=[VMEM, VMEM],
         scratch_shapes=[
-            pltpu.VMEM((6,) + sums.shape, jnp.float32),
+            pltpu.VMEM((6, 1, lanes), jnp.float32),
             pltpu.SemaphoreType.DMA((4,)),
             pltpu.SemaphoreType.DMA((4,)),
         ],
         compiler_params=pltpu.CompilerParams(
-            collective_id=1, has_side_effects=True, vmem_limit_bytes=4 * MIB
+            collective_id=1, has_side_effects=True, vmem_limit_bytes=8 * MIB
         ),
-        name="totals",
-    )(sums)
+        name="product",
+    )(rows, cols, table, extra)
 
 
 STEPS = 6
@@ -539,9 +577,9 @@
 
 
 def body(similarity, block_mask):
-    rows, cols = gather(block_mask, similarity)
-    value, sums = product(rows, cols, *similarity.shape)
-    total = reduce_totals(sums)
+    rows, cols, table = gather(block_mask, similarity)
+    extra = later(rows, cols, table, similarity.shape)
+    value, total = product(rows, cols, table, extra)
     scaling = similarity.shape[0] * lax.axis_size("row")
     return scale(value, total, float(scaling))
 

time: 64.7 us -> 60.7 us (0.938)
  Pallas kernels: 64.5 us -> 60 us
    pallas_call x3, Pallas kernels: 62.2 us -> 57.7 us  [the longest x1 45 us: gather(): pl.pallas_call(gather_kernel, out_shape=[pltpu.VMEM((17, SHARE, BLK), dty...]
where the time goes in v6:
time: 60.7 us; the launch traced here: 60 us
  Pallas kernels  60 us (99%)
    pallas_call x1, Pallas kernels, gather(): pl.pallas_call(gather_kernel, out_shape=[pltpu.VMEM((17, SHARE, BLK), dty...  45 us
    pallas_call x1, Pallas kernels, product(): pl.pallas_call(product_kernel, out_shape=[pltpu.VMEM(extra.shape, jnp.flo...  10.3 us
    pallas_call x1, Pallas kernels, later(): pl.pallas_call(later_kernel, out_shape=pltpu.VMEM(shape, jnp.float32), in...  2.34 us
    pallas_call x1, Pallas kernels, scale(): pl.pallas_call(functools.partial(scale_kernel, scaling), out_shape=jax.Sh...  2.28 us

profile of v6, /device:TPU:0, one launch (start us, length us, event | category | flops | bytes accessed | tf_op | source)
XLA Modules:
  0.0 60.0 jit_solution(7294237465603980879)
XLA Ops:
  0.0 45.0 %gather.1 = (bf16[17,2432,128]{2,1,0:T(8,128)(2,1)S(1)}, bf16[8,2432,128]{2,1,0:T(8,128)(2,1)S(1)}, s32[40,128]{1,0:T(8,128)S(4)}) custom-call(s32[6,12]{1,0:T(8,128)} %bitcast.1, bf16[1536,768]{1,0:T(8,128)(2,1)} %x_ref.1), custom_call_target="tpu_custom_call" | custom-call | tf_op jit(solution)/shard_map/gather/pallas_call | solution.py:356
  45.0 2.3 %later.1.extra_ref = f32[1536,768]{1,0:T(8,128)S(1)} custom-call(bf16[17,2432,128]{2,1,0:T(8,128)(2,1)S(1)} %get-tuple-element.10.rows_ref, bf16[8,2432,128]{2,1,0:T(8,128)(2,1)S(1)} %get-tuple-element.11.cols_ref, s32[40,128]{1,0:T(8,128)S(4)} %get-tuple-element.12.table_ref), custom_call_target="tpu_custom_call" | custom-call | tf_op jit(solution)/shard_map/later/pallas_call | solution.py:458
  47.3 10.3 %product.1 = (f32[1536,768]{1,0:T(8,128)S(1)}, f32[1,768]{1,0:T(1,128)S(1)}) custom-call(bf16[17,2432,128]{2,1,0:T(8,128)(2,1)S(1)} %get-tuple-element.10.rows_ref, bf16[8,2432,128]{2,1,0:T(8,128)(2,1)S(1)} %get-tuple-element.11.cols_ref, s32[40,128]{1,0:T(8,128)S(4)} %get-tuple-element.12.table_ref, f32[1536,768]{1,0:T(8,128)S(1)} %later.1.extra_ref), custom_call_target="tpu_custom_call" | custom-call | tf_op jit(solution)/shard_map/product/pallas_call | solution.py:529
  57.7 2.3 %scale.1 = f32[1536,768]{1,0:T(8,128)} custom-call(f32[1536,768]{1,0:T(8,128)S(1)} %get-tuple-element.13.value_ref, f32[1,768]{1,0:T(1,128)S(1)} %get-tuple-element.14.total_ref), custom_call_target="tpu_custom_call" | custom-call | tf_op jit(solution)/shard_map/scale/pallas_call | solution.py:565

commit v7 on v6

--- a/solution.py
+++ b/solution.py
@@ -294,14 +294,18 @@
     gxp = send(ym_c, ym_c, U1, xp)
     arrived(yxm2, yp_c, U2, xp)
     gxm = send(yp_c, yp_c, U2, xm)
+    sb5 = send(ym_r, ym_r, U1, sib)
+    sb6 = send(yp_r, yp_r, U2, sib)
     arrived(lzp, yp_r, L, lo)
-    arrived(yzm1, yp_r, U1, zp)
-    sb5 = send(yp_r, yp_r, ALL, sib)
+    sb12 = send(yp_r, yp_r, L, sib)
+    arrived(lzm, ym_r, L, lo)
+    sb13 = send(ym_r, ym_r, L, sib)
     arrived(txx, relay.at[2], T, lo)
     uxx = send(relay.at[2], xx_c, T, hi, L)
+    arrived(yzm1, yp_r, U1, zp)
+    sb14 = send(yp_r, yp_r, U1, sib)
     arrived(yzp2, ym_r, U2, zm)
-    arrived(lzm, ym_r, L, lo)
-    sb6 = send(ym_r, ym_r, ALL, sib)
+    sb15 = send(ym_r, ym_r, U2, sib)
     arrived(lzz, yy_r, L, lo)
     sb7 = send(yy_r, yy_r, L, sib)
     arrived(gzp, yy_r, V1, zm)
@@ -324,8 +328,8 @@
     arrived(sb2, rsib(along_z(3)), ALL, sib)
     arrived(sb3, rsib(along_z(1)), ALL, sib)
     arrived(sb4, rsib(along_z(2)), ALL, sib)
-    arrived(sb5, rsib(other(along_z(1))), ALL, sib)
-    arrived(sb6, rsib(other(along_z(3))), ALL, sib)
+    arrived(sb5, rsib(other(along_z(3))), U1, sib)
+    arrived(sb14, rsib(other(along_z(1))), U1, sib)
     arrived(sb8, rsib(other(along_z(2))), V1, sib)
     write_lists(table_v, pair_lists(rows_ref, cols_ref), 0)
     hand = pltpu.make_async_copy(table_v, table_ref, own_sems.at[2])
@@ -337,6 +341,10 @@
     arrived(uxm, ym_c, L, hi)
     arrived(uxx, yy_c, L, hi)
     arrived(gxm, yy_c, U2, xp)
+    arrived(sb6, rsib(other(along_z(1))), U2, sib)
+    arrived(sb12, rsib(other(along_z(1))), L, sib)
+    arrived(sb13, rsib(other(along_z(3))), L, sib)
+    arrived(sb15, rsib(other(along_z(3))), U2, sib)
     arrived(sb7, rsib(other(along_z(2))), L, sib)
     arrived(sb9, rsib(other(along_z(2))), V3, sib)
     arrived(sb10, rsib(other(along_z(2))), V4, sib)
@@ -347,7 +355,7 @@
     hand.wait()
 
 
-COPIES = 53
+COPIES = 57
 
 
 def gather(block_mask, similarity):
@@ -403,40 +411,39 @@
     return ref.reshape(ref.shape[0] * SLOTS, BLK, BLK)
 
 
-def later_kernel(rows_ref, cols_ref, table_ref, extra_ref, table_v, table_s, sem):
+AT_ONCE = 4
+
+
+def later_kernel(rows_ref, cols_ref, table_ref, extra_ref, table_v, table_s, list_s, sem):
     r_ref, c_ref = as_blocks(rows_ref), as_blocks(cols_ref)
-    tiles, wide = extra_ref.shape[0] // BLK, extra_ref.shape[1] // BLK
-
-    def here(i, j):
-        return pl.ds(pl.multiple_of(i * BLK, BLK), BLK), pl.ds(j * BLK, BLK)
-
-    def groups(table, cell):
-        return (jnp.minimum(table[2 * DEPTH, cell], DEPTH) + GROUP - 1) // GROUP
-
-    def add(table, i, j, first):
-        cell = i * wide + j
-
-        @pl.loop(first, groups(table, cell))
+    cells = extra_ref.shape[0] - 1
+
+    def look(cell, found):
+        list_s[found] = cell
+        return found + jnp.where(table_ref[2 * DEPTH, cell] > GROUP, 1, 0)
+
+    found = lax.fori_loop(0, cells, look, jnp.int32(0), unroll=8)
+    for t in range(AT_ONCE):
+        list_s[found + t] = cells
+
+    @pl.loop(0, (found + AT_ONCE - 1) // AT_ONCE)
+    def _(n):
+        for t in range(AT_ONCE):
+            cell = list_s[n * AT_ONCE + t]
+            extra_ref[cell] = group_product(r_ref, c_ref, table_ref, cell, 1)
+
+    def add(table, cell, first):
+        @pl.loop(first, (jnp.minimum(table[2 * DEPTH, cell], DEPTH) + GROUP - 1) // GROUP)
         def _(g):
-            extra_ref[here(i, j)] += group_product(r_ref, c_ref, table, cell, g)
-
-    @pl.loop(0, tiles)
-    def _(i):
-        top = table_ref[2 * DEPTH, i * wide]
-        for j in range(1, wide):
-            top = jnp.maximum(top, table_ref[2 * DEPTH, i * wide + j])
-
-        @pl.when(top > GROUP)
-        def _():
-            for j in range(wide):
-                cell = i * wide + j
-
-                @pl.when(table_ref[2 * DEPTH, cell] > GROUP)
-                def _():
-                    extra_ref[here(i, j)] = group_product(r_ref, c_ref, table_ref, cell, 1)
-                    add(table_ref, i, j, 2)
+            extra_ref[cell] += group_product(r_ref, c_ref, table, cell, g)
 
     most = table_ref[2 * DEPTH + 1, 0]
+
+    @pl.when(most > 2 * GROUP)
+    def _():
+        @pl.loop(0, found)
+        def _(n):
+            add(table_ref, list_s[n], 2)
 
     @pl.loop(1, (most + DEPTH - 1) // DEPTH)
     def _(d):
@@ -445,24 +452,24 @@
         copy.start()
         copy.wait()
 
-        @pl.loop(0, tiles)
-        def _(i):
-            for j in range(wide):
-                add(table_s, i, j, 0)
+        @pl.loop(0, found)
+        def _(n):
+            add(table_s, list_s[n], 0)
 
 
 VMEM, SMEM = pl.BlockSpec(memory_space=pltpu.VMEM), pl.BlockSpec(memory_space=pltpu.SMEM)
 
 
-def later(rows, cols, table, shape):
+def later(rows, cols, table, cells):
     return pl.pallas_call(
         later_kernel,
-        out_shape=pltpu.VMEM(shape, jnp.float32),
+        out_shape=pltpu.VMEM((cells + 1, BLK, BLK), jnp.float32),
         in_specs=[VMEM, VMEM, SMEM],
         out_specs=VMEM,
         scratch_shapes=[
             pltpu.VMEM(table.shape, jnp.int32),
             pltpu.SMEM(table.shape, jnp.int32),
+            pltpu.SMEM((BLK,), jnp.int32),
             pltpu.SemaphoreType.DMA(()),
         ],
         compiler_params=pltpu.CompilerParams(vmem_limit_bytes=8 * MIB),
@@ -474,11 +481,9 @@
     rows_ref, cols_ref, table_ref, extra_ref, out_ref, total_ref, slots, send_sems, recv_sems
 ):
     row, col, layer = (lax.axis_index(a) for a in ("row", "col", "layer"))
-    high, x = row // 4, row % 4
-    near = [(4 * high + (x + s) % 4, col, layer) for s in range(1, 4)]
-    far = (4 * (1 - high) + x, col, layer)
+    peers = [((row + s) % 8, col, layer) for s in range(1, 8)]
     barrier = pltpu.get_barrier_semaphore()
-    for peer in near + [far]:
+    for peer in peers:
         pl.semaphore_signal(barrier, inc=1, device_id=peer, device_id_type=MESH)
 
     r_ref, c_ref = as_blocks(rows_ref), as_blocks(cols_ref)
@@ -491,7 +496,7 @@
             cell = i * wide + j
             value = group_product(r_ref, c_ref, table_ref, cell, 0)
             has_more = jnp.full((BLK, BLK), table_ref[2 * DEPTH, cell], jnp.int32) > GROUP
-            value = value + jnp.where(has_more, extra_ref[lines, pl.ds(j * BLK, BLK)], 0.0)
+            value = value + jnp.where(has_more, extra_ref[cell], 0.0)
             value = value * value
             out_ref[lines, pl.ds(j * BLK, BLK)] = value
             out.append(sums[j] + jnp.sum(value.reshape(BLK // 8, 8, BLK), axis=0))
@@ -499,42 +504,40 @@
 
     sums = tuple(jnp.zeros((8, BLK), jnp.float32) for _ in range(wide))
     sums = lax.fori_loop(0, tiles, one_row, sums, unroll=3)
-    slots[x] = jnp.concatenate([jnp.sum(v, axis=0, keepdims=True) for v in sums], 1)
-    pl.semaphore_wait(barrier, 4)
-
-    def swap(k, src, dst, peer):
-        return pltpu.make_async_remote_copy(
-            src_ref=slots.at[src],
-            dst_ref=slots.at[dst],
+    slots[row] = jnp.concatenate([jnp.sum(v, axis=0, keepdims=True) for v in sums], 1)
+    pl.semaphore_wait(barrier, 7)
+    copies = [
+        pltpu.make_async_remote_copy(
+            src_ref=slots.at[row],
+            dst_ref=slots.at[row],
             send_sem=send_sems.at[k],
             recv_sem=recv_sems.at[k],
             device_id=peer,
             device_id_type=MESH,
         )
-
-    copies = [swap(k, x, x, peer) for k, peer in enumerate(near)]
+        for k, peer in enumerate(peers)
+    ]
     for copy in copies:
         copy.start()
     for copy in copies:
         copy.wait()
-    slots[4] = (slots[0] + slots[1]) + (slots[2] + slots[3])
-    copy = swap(3, 4, 5, far)
-    copy.start()
-    copy.wait()
-    total_ref[...] = slots[4] + slots[5]
-
-
-def product(rows, cols, table, extra):
-    lanes = extra.shape[1]
+    total = slots[0]
+    for q in range(1, 8):
+        total = total + slots[q]
+    total_ref[...] = total
+
+
+def product(rows, cols, table, extra, shape):
+    lanes = shape[1]
     return pl.pallas_call(
         product_kernel,
-        out_shape=[pltpu.VMEM(extra.shape, jnp.float32), pltpu.VMEM((1, lanes), jnp.float32)],
+        out_shape=[pltpu.VMEM(shape, jnp.float32), pltpu.VMEM((1, lanes), jnp.float32)],
         in_specs=[VMEM, VMEM, SMEM, VMEM],
         out_specs=[VMEM, VMEM],
         scratch_shapes=[
-            pltpu.VMEM((6, 1, lanes), jnp.float32),
-            pltpu.SemaphoreType.DMA((4,)),
-            pltpu.SemaphoreType.DMA((4,)),
+            pltpu.VMEM((8, 1, lanes), jnp.float32),
+            pltpu.SemaphoreType.DMA((7,)),
+            pltpu.SemaphoreType.DMA((7,)),
         ],
         compiler_params=pltpu.CompilerParams(
             collective_id=1, has_side_effects=True, vmem_limit_bytes=8 * MIB
@@ -578,8 +581,8 @@
 
 def body(similarity, block_mask):
     rows, cols, table = gather(block_mask, similarity)
-    extra = later(rows, cols, table, similarity.shape)
-    value, total = product(rows, cols, table, extra)
+    extra = later(rows, cols, table, block_mask.size)
+    value, total = product(rows, cols, table, extra, similarity.shape)
     scaling = similarity.shape[0] * lax.axis_size("row")
     return scale(value, total, float(scaling))
 

time: 60.7 us -> 58.6 us (0.965)
  Pallas kernels: 60 us -> 57.4 us
    pallas_call x2, Pallas kernels: 12.7 us -> 10 us  [the longest x1 9.11 us: product(): pl.pallas_call(product_kernel, out_shape=[pltpu.VMEM(shape, jnp.float32),...]
where the time goes in v7:
time: 58.6 us; the launch traced here: 57.4 us
  Pallas kernels  57.4 us (98%)
    pallas_call x1, Pallas kernels, gather(): pl.pallas_call(gather_kernel, out_shape=[pltpu.VMEM((17, SHARE, BLK), dty...  45.1 us
    pallas_call x1, Pallas kernels, product(): pl.pallas_call(product_kernel, out_shape=[pltpu.VMEM(shape, jnp.float32),...  9.11 us
    pallas_call x1, Pallas kernels, scale(): pl.pallas_call(functools.partial(scale_kernel, scaling), out_shape=jax.Sh...  2.28 us

profile of v7, /device:TPU:0, one launch (start us, length us, event | category | flops | bytes accessed | tf_op | source)
XLA Modules:
  0.0 57.4 jit_solution(7605043490351030486)
XLA Ops:
  0.0 45.1 %gather.1 = (bf16[17,2432,128]{2,1,0:T(8,128)(2,1)S(1)}, bf16[8,2432,128]{2,1,0:T(8,128)(2,1)S(1)}, s32[40,128]{1,0:T(8,128)S(4)}) custom-call(s32[6,12]{1,0:T(8,128)} %bitcast.1, bf16[1536,768]{1,0:T(8,128)(2,1)} %x_ref.1), custom_call_target="tpu_custom_call" | custom-call | tf_op jit(solution)/shard_map/gather/pallas_call | solution.py:364
  45.1 0.9 %later.1.extra_ref = f32[73,128,128]{2,1,0:T(8,128)S(1)} custom-call(bf16[17,2432,128]{2,1,0:T(8,128)(2,1)S(1)} %get-tuple-element.10.rows_ref, bf16[8,2432,128]{2,1,0:T(8,128)(2,1)S(1)} %get-tuple-element.11.cols_ref, s32[40,128]{1,0:T(8,128)S(4)} %get-tuple-element.12.table_ref), custom_call_target="tpu_custom_call" | custom-call | tf_op jit(solution)/shard_map/later/pallas_call | solution.py:464
  46.0 9.1 %product.1 = (f32[1536,768]{1,0:T(8,128)S(1)}, f32[1,768]{1,0:T(1,128)S(1)}) custom-call(bf16[17,2432,128]{2,1,0:T(8,128)(2,1)S(1)} %get-tuple-element.10.rows_ref, bf16[8,2432,128]{2,1,0:T(8,128)(2,1)S(1)} %get-tuple-element.11.cols_ref, s32[40,128]{1,0:T(8,128)S(4)} %get-tuple-element.12.table_ref, f32[73,128,128]{2,1,0:T(8,128)S(1)} %later.1.extra_ref), custom_call_target="tpu_custom_call" | custom-call | tf_op jit(solution)/shard_map/product/pallas_call | solution.py:532
  55.1 2.3 %scale.1 = f32[1536,768]{1,0:T(8,128)} custom-call(f32[1536,768]{1,0:T(8,128)S(1)} %get-tuple-element.13.value_ref, f32[1,768]{1,0:T(1,128)S(1)} %get-tuple-element.14.total_ref), custom_call_target="tpu_custom_call" | custom-call | tf_op jit(solution)/shard_map/scale/pallas_call | solution.py:568

commit v8 on v7

--- a/solution.py
+++ b/solution.py
@@ -20,8 +20,10 @@
 MESH = pl.DeviceIdType.MESH
 
 
-def pack_share(mask_ref, x_ref, x_v, share, place_v, place_s, sems):
+def pack_share(mask_ref, x_ref, mask_s, x_v, share, place_v, place_s, signal, sems):
     cols, rows = mask_ref.shape
+    fetch = pltpu.make_async_copy(mask_ref, mask_s, sems.at[cols + 1])
+    fetch.start()
     strips = x_v.reshape(cols * rows * BLK, BLK)
     loads = [
         pltpu.make_async_copy(
@@ -33,6 +35,7 @@
     ]
     for load in loads:
         load.start()
+    signal()
     sub = lax.broadcasted_iota(jnp.int32, (HEAD, BLK), 0)
     lane = lax.broadcasted_iota(jnp.int32, (HEAD, BLK), 1)
     lane_row = (lane * 43) >> 8
@@ -42,11 +45,12 @@
     def find(i, carry):
         count, place = carry
         for j in range(cols):
-            here = mask_ref[j, i]
+            here = mask_s[j, i]
             place = place + jnp.where(lane8 == count, here * (j * rows + i), 0)
             count = count + here
         return count, place
 
+    fetch.wait()
     zero = jnp.int32(0)
     _, place = lax.fori_loop(0, rows, find, (zero, jnp.zeros((8, BLK), jnp.int32)), unroll=3)
     place_v[...] = place
@@ -57,7 +61,7 @@
         count, head = carry
         below = 8 + jnp.where(i < cols, i, i - cols + 8)
         for j in range(cols):
-            here = mask_ref[j, i]
+            here = mask_s[j, i]
             cell = ((sub == j) & (lane_row == i)) | ((sub == below) & (lane_col == j))
             head = head + jnp.where(cell, here * (count + 1), 0)
             count = count + here
@@ -125,6 +129,7 @@
     rows_ref,
     cols_ref,
     table_ref,
+    mask_s,
     x_v,
     share_ref,
     relay,
@@ -155,9 +160,12 @@
     sib = (row, col, 1 - layer)
 
     barrier = pltpu.get_barrier_semaphore()
-    for peer in (zp, zm, xp, xm, lo, hi, sib):
-        pl.semaphore_signal(barrier, inc=1, device_id=peer, device_id_type=MESH)
-    pack_share(mask_ref, x_ref, x_v, share_ref, place_v, place_s, pack_sems)
+
+    def signal():
+        for peer in (zp, zm, xp, xm, lo, hi, sib):
+            pl.semaphore_signal(barrier, inc=1, device_id=peer, device_id_type=MESH)
+
+    pack_share(mask_ref, x_ref, mask_s, x_v, share_ref, place_v, place_s, signal, pack_sems)
     pl.semaphore_wait(barrier, 7)
 
     ALL = span(0, MAXNZ)
@@ -368,16 +376,14 @@
             pltpu.VMEM((8, SHARE, BLK), dtype),
             pltpu.SMEM((2 * DEPTH + 8, BLK), jnp.int32),
         ],
-        in_specs=[
-            pl.BlockSpec(memory_space=pltpu.SMEM),
-            pl.BlockSpec(memory_space=pl.ANY),
-        ],
+        in_specs=[pl.BlockSpec(memory_space=pltpu.HBM)] * 2,
         out_specs=[
             pl.BlockSpec(memory_space=pltpu.VMEM),
             pl.BlockSpec(memory_space=pltpu.VMEM),
             pl.BlockSpec(memory_space=pltpu.SMEM),
         ],
         scratch_shapes=[
+            pltpu.SMEM(block_mask.shape[::-1], jnp.int32),
             pltpu.VMEM((cells, BLK, BLK), dtype),
             pltpu.VMEM((SHARE, BLK), dtype),
             pltpu.VMEM((3, LAST * BLK, BLK), dtype),
@@ -386,7 +392,7 @@
             pltpu.SemaphoreType.DMA((COPIES,)),
             pltpu.SemaphoreType.DMA((COPIES,)),
             pltpu.SemaphoreType.DMA((3,)),
-            pltpu.SemaphoreType.DMA((7,)),
+            pltpu.SemaphoreType.DMA((8,)),
             pltpu.VMEM((2 * DEPTH + 8, BLK), jnp.int32),
         ],
         compiler_params=pltpu.CompilerParams(
@@ -551,11 +557,11 @@
 
 def scale_kernel(scaling, value_ref, total_ref, out_ref, staged, sems):
     step = staged.shape[1]
-    total = total_ref[...]
+    factor = scaling / total_ref[...]
     copies = []
     for t in range(STEPS):
         here = pl.ds(t * step, step)
-        staged[t] = scaling * value_ref[here, :] / total
+        staged[t] = value_ref[here, :] * factor
         copy = pltpu.make_async_copy(staged.at[t], out_ref.at[here], sems.at[t])
         copy.start()
         copies.append(copy)

time: 58.6 us -> 57.8 us (0.986)
  the two profiles are of different devices: /device:TPU:0 before, /device:TPU:1 now
where the time goes in v8:
time: 57.8 us; the launch traced here: 57.6 us
  Pallas kernels  57.6 us (100%)
    pallas_call x1, Pallas kernels, gather(): pl.pallas_call(gather_kernel, out_shape=[pltpu.VMEM((17, SHARE, BLK), dty...  44.8 us
    pallas_call x1, Pallas kernels, product(): pl.pallas_call(product_kernel, out_shape=[pltpu.VMEM(shape, jnp.float32),...  8.18 us
    pallas_call x1, Pallas kernels, later(): pl.pallas_call(later_kernel, out_shape=pltpu.VMEM((cells + 1, BLK, BLK),...  2.32 us
    pallas_call x1, Pallas kernels, scale(): pl.pallas_call(functools.partial(scale_kernel, scaling), out_shape=jax.Sh...  2.29 us

profile of v8, /device:TPU:1, one launch (start us, length us, event | category | flops | bytes accessed | tf_op | source)
XLA Modules:
  0.0 57.6 jit_solution(782796556979250122)
XLA Ops:
  0.0 44.8 %gather.1 = (bf16[17,2432,128]{2,1,0:T(8,128)(2,1)S(1)}, bf16[8,2432,128]{2,1,0:T(8,128)(2,1)S(1)}, s32[40,128]{1,0:T(8,128)S(4)}) custom-call(s32[6,12]{1,0:T(8,128)} %bitcast.1, bf16[1536,768]{1,0:T(8,128)(2,1)} %x_ref.1), custom_call_target="tpu_custom_call" | custom-call | tf_op jit(solution)/shard_map/gather/pallas_call | solution.py:372
  44.8 2.3 %later.1.extra_ref = f32[73,128,128]{2,1,0:T(8,128)S(1)} custom-call(bf16[17,2432,128]{2,1,0:T(8,128)(2,1)S(1)} %get-tuple-element.10.rows_ref, bf16[8,2432,128]{2,1,0:T(8,128)(2,1)S(1)} %get-tuple-element.11.cols_ref, s32[40,128]{1,0:T(8,128)S(4)} %get-tuple-element.12.table_ref), custom_call_target="tpu_custom_call" | custom-call | tf_op jit(solution)/shard_map/later/pallas_call | solution.py:470
  47.2 8.2 %product.1 = (f32[1536,768]{1,0:T(8,128)S(1)}, f32[1,768]{1,0:T(1,128)S(1)}) custom-call(bf16[17,2432,128]{2,1,0:T(8,128)(2,1)S(1)} %get-tuple-element.10.rows_ref, bf16[8,2432,128]{2,1,0:T(8,128)(2,1)S(1)} %get-tuple-element.11.cols_ref, s32[40,128]{1,0:T(8,128)S(4)} %get-tuple-element.12.table_ref, f32[73,128,128]{2,1,0:T(8,128)S(1)} %later.1.extra_ref), custom_call_target="tpu_custom_call" | custom-call | tf_op jit(solution)/shard_map/product/pallas_call | solution.py:538
  55.4 2.3 %scale.1 = f32[1536,768]{1,0:T(8,128)} custom-call(f32[1536,768]{1,0:T(8,128)S(1)} %get-tuple-element.13.value_ref, f32[1,768]{1,0:T(1,128)S(1)} %get-tuple-element.14.total_ref), custom_call_target="tpu_custom_call" | custom-call | tf_op jit(solution)/shard_map/scale/pallas_call | solution.py:574

commit v9 on v8

--- a/solution.py
+++ b/solution.py
@@ -16,6 +16,8 @@
 TOP = BLK - HEAD
 GROUP = 4
 DEPTH = 16
+FIELD = 256
+COUNT = 512 * FIELD
 MIB = 1 << 20
 MESH = pl.DeviceIdType.MESH
 
@@ -97,21 +99,27 @@
     place_r = (line >> 3) * SLOTS + hr.astype(jnp.int32)
     place_c = (line >> 4) * SLOTS + hc.astype(jnp.int32)
     count = jnp.sum(both, axis=0, keepdims=True).astype(jnp.int32)
-    return rank, place_r, place_c, count
+    return rank, place_r * FIELD + place_c, count
 
 
 def write_lists(table_v, lists, done):
-    rank, place_r, place_c, count = lists
+    rank, place, count = lists
+    most = jnp.max(count, axis=1, keepdims=True)
+    lane = lax.broadcasted_iota(jnp.int32, count.shape, 1)
     for p in range(DEPTH):
-        at = rank == done + p
-        some = count > done + p
-        first = jnp.sum(jnp.where(at, place_r, 0), axis=0, keepdims=True)
-        second = jnp.sum(jnp.where(at, place_c, 0), axis=0, keepdims=True)
-        table_v[pl.ds(p, 1), :] = jnp.where(some, first, 16 * SLOTS)
-        table_v[pl.ds(DEPTH + p, 1), :] = jnp.where(some, second, 1)
-    most = jnp.max(count, axis=1, keepdims=True)
-    table_v[pl.ds(2 * DEPTH, 1), :] = count - done
-    table_v[pl.ds(2 * DEPTH + 1, 1), :] = jnp.broadcast_to(most, count.shape)
+        one = jnp.sum(jnp.where(rank == done + p, place, 0), axis=0, keepdims=True)
+        one = jnp.where(count > done + p, one, IDLE)
+        if p == 0:
+            length = jnp.where(lane == BLK - 1, most, jnp.maximum(count - done, 0))
+            one = one + COUNT * length
+        table_v[pl.ds(p, 1), :] = one
+
+
+IDLE = 16 * SLOTS * FIELD + 1
+
+
+def length_of(table, cell):
+    return table[0, cell] >> 17
 
 
 LAST = 5
@@ -299,7 +307,8 @@
     gzm = send(yp_r, yp_r, V3, zm)
     gzn = send(yp_r, yp_r, V4, zm)
     arrived(yxp1, ym_c, U1, xm)
-    gxp = send(ym_c, ym_c, U1, xp)
+    gxp = send(ym_c, ym_c, V1, xp)
+    gxq = send(ym_c, ym_c, V2, xp)
     arrived(yxm2, yp_c, U2, xp)
     gxm = send(yp_c, yp_c, U2, xm)
     sb5 = send(ym_r, ym_r, U1, sib)
@@ -316,25 +325,20 @@
     sb15 = send(ym_r, ym_r, U2, sib)
     arrived(lzz, yy_r, L, lo)
     sb7 = send(yy_r, yy_r, L, sib)
-    arrived(gzp, yy_r, V1, zm)
-    sb8 = send(yy_r, yy_r, V1, sib)
-    arrived(gzm, yy_r, V3, zp)
-    sb9 = send(yy_r, yy_r, V3, sib)
-    arrived(gzn, yy_r, V4, zp)
-    sb10 = send(yy_r, yy_r, V4, sib)
-    arrived(gzq, yy_r, V2, zm)
-    sb11 = send(yy_r, yy_r, V2, sib)
-
     for copy in keep:
         copy.wait()
     arrived(xm1, xp_c, H1, xp)
     arrived(fxp, xx_c, H1, xm)
     arrived(yxm1, yp_c, U1, xp)
-    arrived(gxp, yy_c, U1, xm)
     arrived(sb0, rsib(col), ALL, sib)
     arrived(sb1, rsib(mate), ALL, sib)
     arrived(sb2, rsib(along_z(3)), ALL, sib)
     arrived(sb3, rsib(along_z(1)), ALL, sib)
+    arrived(gzp, yy_r, V1, zm)
+    sb8 = send(yy_r, yy_r, V1, sib)
+    arrived(gzm, yy_r, V3, zp)
+    sb9 = send(yy_r, yy_r, V3, sib)
+    arrived(gxp, yy_c, V1, xm)
     arrived(sb4, rsib(along_z(2)), ALL, sib)
     arrived(sb5, rsib(other(along_z(3))), U1, sib)
     arrived(sb14, rsib(other(along_z(1))), U1, sib)
@@ -342,6 +346,10 @@
     write_lists(table_v, pair_lists(rows_ref, cols_ref), 0)
     hand = pltpu.make_async_copy(table_v, table_ref, own_sems.at[2])
     hand.start()
+    arrived(gzn, yy_r, V4, zp)
+    sb10 = send(yy_r, yy_r, V4, sib)
+    arrived(gzq, yy_r, V2, zm)
+    sb11 = send(yy_r, yy_r, V2, sib)
 
     arrived(hi3, y_c, L, hi)
     arrived(yxp2, ym_c, U2, xm)
@@ -349,6 +357,7 @@
     arrived(uxm, ym_c, L, hi)
     arrived(uxx, yy_c, L, hi)
     arrived(gxm, yy_c, U2, xp)
+    arrived(gxq, yy_c, V2, xm)
     arrived(sb6, rsib(other(along_z(1))), U2, sib)
     arrived(sb12, rsib(other(along_z(1))), L, sib)
     arrived(sb13, rsib(other(along_z(3))), L, sib)
@@ -363,7 +372,7 @@
     hand.wait()
 
 
-COPIES = 57
+COPIES = 58
 
 
 def gather(block_mask, similarity):
@@ -374,7 +383,7 @@
         out_shape=[
             pltpu.VMEM((17, SHARE, BLK), dtype),
             pltpu.VMEM((8, SHARE, BLK), dtype),
-            pltpu.SMEM((2 * DEPTH + 8, BLK), jnp.int32),
+            pltpu.SMEM((DEPTH, BLK), jnp.int32),
         ],
         in_specs=[pl.BlockSpec(memory_space=pltpu.HBM)] * 2,
         out_specs=[
@@ -393,7 +402,7 @@
             pltpu.SemaphoreType.DMA((COPIES,)),
             pltpu.SemaphoreType.DMA((3,)),
             pltpu.SemaphoreType.DMA((8,)),
-            pltpu.VMEM((2 * DEPTH + 8, BLK), jnp.int32),
+            pltpu.VMEM((DEPTH, BLK), jnp.int32),
         ],
         compiler_params=pltpu.CompilerParams(
             collective_id=0, has_side_effects=True, vmem_limit_bytes=44 * MIB
@@ -403,13 +412,14 @@
 
 
 def group_product(r_ref, c_ref, table, cell, g):
+    words = [table[g * GROUP + t, cell] for t in range(GROUP)]
     return sum(
         jnp.dot(
-            r_ref[table[p, cell]],
-            c_ref[table[DEPTH + p, cell]],
+            r_ref[(word >> 8) & 511],
+            c_ref[word & 255],
             preferred_element_type=jnp.float32,
         )
-        for p in [g * GROUP + t for t in range(GROUP)]
+        for word in words
     )
 
 
@@ -426,7 +436,7 @@
 
     def look(cell, found):
         list_s[found] = cell
-        return found + jnp.where(table_ref[2 * DEPTH, cell] > GROUP, 1, 0)
+        return found + jnp.where(length_of(table_ref, cell) > GROUP, 1, 0)
 
     found = lax.fori_loop(0, cells, look, jnp.int32(0), unroll=8)
     for t in range(AT_ONCE):
@@ -439,11 +449,11 @@
             extra_ref[cell] = group_product(r_ref, c_ref, table_ref, cell, 1)
 
     def add(table, cell, first):
-        @pl.loop(first, (jnp.minimum(table[2 * DEPTH, cell], DEPTH) + GROUP - 1) // GROUP)
+        @pl.loop(first, (jnp.minimum(length_of(table, cell), DEPTH) + GROUP - 1) // GROUP)
         def _(g):
             extra_ref[cell] += group_product(r_ref, c_ref, table, cell, g)
 
-    most = table_ref[2 * DEPTH + 1, 0]
+    most = length_of(table_ref, BLK - 1)
 
     @pl.when(most > 2 * GROUP)
     def _():
@@ -501,7 +511,7 @@
         for j in range(wide):
             cell = i * wide + j
             value = group_product(r_ref, c_ref, table_ref, cell, 0)
-            has_more = jnp.full((BLK, BLK), table_ref[2 * DEPTH, cell], jnp.int32) > GROUP
+            has_more = jnp.full((BLK, BLK), length_of(table_ref, cell), jnp.int32) > GROUP
             value = value + jnp.where(has_more, extra_ref[cell], 0.0)
             value = value * value
             out_ref[lines, pl.ds(j * BLK, BLK)] = value
@@ -509,7 +519,7 @@
         return tuple(out)
 
     sums = tuple(jnp.zeros((8, BLK), jnp.float32) for _ in range(wide))
-    sums = lax.fori_loop(0, tiles, one_row, sums, unroll=3)
+    sums = lax.fori_loop(0, tiles, one_row, sums, unroll=6)
     slots[row] = jnp.concatenate([jnp.sum(v, axis=0, keepdims=True) for v in sums], 1)
     pl.semaphore_wait(barrier, 7)
     copies = [

time: 57.8 us -> 57.5 us (level)
  the two profiles are of different devices: /device:TPU:1 before, /device:TPU:0 now
where the time goes in v9:
time: 57.5 us; the launch traced here: 57.3 us
  Pallas kernels  57.3 us (100%)
    pallas_call x1, Pallas kernels, gather(): pl.pallas_call(gather_kernel, out_shape=[pltpu.VMEM((17, SHARE, BLK), dty...  44.3 us
    pallas_call x1, Pallas kernels, product(): pl.pallas_call(product_kernel, out_shape=[pltpu.VMEM(shape, jnp.float32),...  10.1 us
    pallas_call x1, Pallas kernels, scale(): pl.pallas_call(functools.partial(scale_kernel, scaling), out_shape=jax.Sh...  2.29 us

profile of v9, /device:TPU:0, one launch (start us, length us, event | category | flops | bytes accessed | tf_op | source)
XLA Modules:
  0.0 57.3 jit_solution(6130953669556818516)
XLA Ops:
  0.0 44.3 %gather.1 = (bf16[17,2432,128]{2,1,0:T(8,128)(2,1)S(1)}, bf16[8,2432,128]{2,1,0:T(8,128)(2,1)S(1)}, s32[16,128]{1,0:T(8,128)S(4)}) custom-call(s32[6,12]{1,0:T(8,128)} %bitcast.1, bf16[1536,768]{1,0:T(8,128)(2,1)} %x_ref.1), custom_call_target="tpu_custom_call" | custom-call | tf_op jit(solution)/shard_map/gather/pallas_call | solution.py:381
  44.4 0.5 later.1.extra_ref
  44.9 10.1 %product.1 = (f32[1536,768]{1,0:T(8,128)S(1)}, f32[1,768]{1,0:T(1,128)S(1)}) custom-call(bf16[17,2432,128]{2,1,0:T(8,128)(2,1)S(1)} %get-tuple-element.10.rows_ref, bf16[8,2432,128]{2,1,0:T(8,128)(2,1)S(1)} %get-tuple-element.11.cols_ref, s32[16,128]{1,0:T(8,128)S(4)} %get-tuple-element.12.table_ref, f32[73,128,128]{2,1,0:T(8,128)S(1)} %later.1.extra_ref), custom_call_target="tpu_custom_call" | custom-call | tf_op jit(solution)/shard_map/product/pallas_call | solution.py:548
  55.0 2.3 %scale.1 = f32[1536,768]{1,0:T(8,128)} custom-call(f32[1536,768]{1,0:T(8,128)S(1)} %get-tuple-element.13.value_ref, f32[1,768]{1,0:T(1,128)S(1)} %get-tuple-element.14.total_ref), custom_call_target="tpu_custom_call" | custom-call | tf_op jit(solution)/shard_map/scale/pallas_call | solution.py:584

commit v10 on v9

--- a/solution.py
+++ b/solution.py
@@ -122,7 +122,8 @@
     return table[0, cell] >> 17
 
 
-LAST = 5
+LAST_R = 5
+LAST_C = 4
 SPLIT = 7
 
 
@@ -183,11 +184,12 @@
         pltpu.make_async_copy(share_ref.at[ALL], cols_ref.at[row].at[ALL], own_sems.at[1]),
     ]
 
-    EARLY = MAXNZ - LAST
+    EARLY, EARLY_C = MAXNZ - LAST_R, MAXNZ - LAST_C
     H1, H2 = span(0, HALF), span(HALF, MAXNZ)
     U1, U2, L = span(0, SPLIT), span(SPLIT, EARLY), span(EARLY, MAXNZ)
     V1, V2, V3, V4 = span(0, 4), span(4, SPLIT), span(SPLIT, 10), span(10, EARLY)
-    T = pl.ds(0, LAST * BLK)
+    W2, K = span(SPLIT, EARLY_C), span(EARLY_C, MAXNZ)
+    T = pl.ds(0, LAST_C * BLK)
     started = []
     waited = set()
 
@@ -265,7 +267,7 @@
     fxp = send(xm_c, xm_c, H1, xp)
     arrived(xm2, xp_c, H2, xp)
     fxm = send(xp_c, xp_c, H2, xm)
-    txp = send(xp_c, relay.at[0], L, lo, T)
+    txp = send(xp_c, relay.at[0], K, lo, T)
     lzp = send(zp_r, zp_r, L, lo)
     arrived(lo2, y_r, U2, lo)
     hi2 = send(y_r, own_c, U2, hi)
@@ -280,25 +282,26 @@
 
     arrived(zp2, zm_r, H2, zm)
     arrived(xp2, xm_c, H2, xm)
-    txm = send(xm_c, relay.at[1], L, lo, T)
+    txm = send(xm_c, relay.at[1], K, lo, T)
     lzm = send(zm_r, zm_r, L, lo)
     sb2 = send(zm_r, zm_r, ALL, sib)
     arrived(zm1, zp_r, H1, zp)
     sb3 = send(zp_r, zp_r, ALL, sib)
     arrived(hi2, y_c, U2, hi)
-    yxm2 = send(y_c, y_c, U2, xm)
-    yxp2 = send(y_c, y_c, U2, xp)
+    arrived(hi3, y_c, L, hi)
+    yxm2 = send(y_c, y_c, W2, xm)
+    yxp2 = send(y_c, y_c, W2, xp)
     yxm1 = send(y_c, y_c, U1, xm)
     arrived(txp, relay.at[0], T, lo)
-    uxp = send(relay.at[0], xp_c, T, hi, L)
+    uxp = send(relay.at[0], xp_c, T, hi, K)
     arrived(fxm, xx_c, H2, xp)
-    txx = send(xx_c, relay.at[2], L, lo, T)
+    txx = send(xx_c, relay.at[2], K, lo, T)
     arrived(fzm, zz_r, H2, zp)
     lzz = send(zz_r, zz_r, L, lo)
     arrived(fzp, zz_r, H1, zm)
     sb4 = send(zz_r, zz_r, ALL, sib)
     arrived(txm, relay.at[1], T, lo)
-    uxm = send(relay.at[1], xm_c, T, hi, L)
+    uxm = send(relay.at[1], xm_c, T, hi, K)
 
     arrived(yzp1, ym_r, U1, zm)
     gzp = send(ym_r, ym_r, V1, zp)
@@ -309,8 +312,8 @@
     arrived(yxp1, ym_c, U1, xm)
     gxp = send(ym_c, ym_c, V1, xp)
     gxq = send(ym_c, ym_c, V2, xp)
-    arrived(yxm2, yp_c, U2, xp)
-    gxm = send(yp_c, yp_c, U2, xm)
+    arrived(yxm2, yp_c, W2, xp)
+    gxm = send(yp_c, yp_c, W2, xm)
     sb5 = send(ym_r, ym_r, U1, sib)
     sb6 = send(yp_r, yp_r, U2, sib)
     arrived(lzp, yp_r, L, lo)
@@ -318,7 +321,7 @@
     arrived(lzm, ym_r, L, lo)
     sb13 = send(ym_r, ym_r, L, sib)
     arrived(txx, relay.at[2], T, lo)
-    uxx = send(relay.at[2], xx_c, T, hi, L)
+    uxx = send(relay.at[2], xx_c, T, hi, K)
     arrived(yzm1, yp_r, U1, zp)
     sb14 = send(yp_r, yp_r, U1, sib)
     arrived(yzp2, ym_r, U2, zm)
@@ -351,12 +354,11 @@
     arrived(gzq, yy_r, V2, zm)
     sb11 = send(yy_r, yy_r, V2, sib)
 
-    arrived(hi3, y_c, L, hi)
-    arrived(yxp2, ym_c, U2, xm)
-    arrived(uxp, yp_c, L, hi)
-    arrived(uxm, ym_c, L, hi)
-    arrived(uxx, yy_c, L, hi)
-    arrived(gxm, yy_c, U2, xp)
+    arrived(yxp2, ym_c, W2, xm)
+    arrived(uxp, yp_c, K, hi)
+    arrived(uxm, ym_c, K, hi)
+    arrived(uxx, yy_c, K, hi)
+    arrived(gxm, yy_c, W2, xp)
     arrived(gxq, yy_c, V2, xm)
     arrived(sb6, rsib(other(along_z(1))), U2, sib)
     arrived(sb12, rsib(other(along_z(1))), L, sib)
@@ -395,7 +397,7 @@
             pltpu.SMEM(block_mask.shape[::-1], jnp.int32),
             pltpu.VMEM((cells, BLK, BLK), dtype),
             pltpu.VMEM((SHARE, BLK), dtype),
-            pltpu.VMEM((3, LAST * BLK, BLK), dtype),
+            pltpu.VMEM((3, LAST_C * BLK, BLK), dtype),
             pltpu.VMEM((8, BLK), jnp.int32),
             pltpu.SMEM((8, BLK), jnp.int32),
             pltpu.SemaphoreType.DMA((COPIES,)),

time: 57.5 us -> 57 us (level)
  no operation moved by 1% of the time
where the time goes in v10:
time: 57 us; the launch traced here: 56.9 us
  Pallas kernels  56.9 us (100%)
    pallas_call x1, Pallas kernels, gather(): pl.pallas_call(gather_kernel, out_shape=[pltpu.VMEM((17, SHARE, BLK), dty...  44 us
    pallas_call x1, Pallas kernels, product(): pl.pallas_call(product_kernel, out_shape=[pltpu.VMEM(shape, jnp.float32),...  10 us
    pallas_call x1, Pallas kernels, scale(): pl.pallas_call(functools.partial(scale_kernel, scaling), out_shape=jax.Sh...  2.29 us

profile of v10, /device:TPU:0, one launch (start us, length us, event | category | flops | bytes accessed | tf_op | source)
XLA Modules:
  0.0 56.9 jit_solution(18269537232985385746)
XLA Ops:
  0.0 44.0 %gather.1 = (bf16[17,2432,128]{2,1,0:T(8,128)(2,1)S(1)}, bf16[8,2432,128]{2,1,0:T(8,128)(2,1)S(1)}, s32[16,128]{1,0:T(8,128)S(4)}) custom-call(s32[6,12]{1,0:T(8,128)} %bitcast.1, bf16[1536,768]{1,0:T(8,128)(2,1)} %x_ref.1), custom_call_target="tpu_custom_call" | custom-call | tf_op jit(solution)/shard_map/gather/pallas_call | solution.py:383
  44.0 0.5 later.1.extra_ref
  44.6 10.0 %product.1 = (f32[1536,768]{1,0:T(8,128)S(1)}, f32[1,768]{1,0:T(1,128)S(1)}) custom-call(bf16[17,2432,128]{2,1,0:T(8,128)(2,1)S(1)} %get-tuple-element.10.rows_ref, bf16[8,2432,128]{2,1,0:T(8,128)(2,1)S(1)} %get-tuple-element.11.cols_ref, s32[16,128]{1,0:T(8,128)S(4)} %get-tuple-element.12.table_ref, f32[73,128,128]{2,1,0:T(8,128)S(1)} %later.1.extra_ref), custom_call_target="tpu_custom_call" | custom-call | tf_op jit(solution)/shard_map/product/pallas_call | solution.py:550
  54.6 2.3 %scale.1 = f32[1536,768]{1,0:T(8,128)} custom-call(f32[1536,768]{1,0:T(8,128)S(1)} %get-tuple-element.13.value_ref, f32[1,768]{1,0:T(1,128)S(1)} %get-tuple-element.14.total_ref), custom_call_target="tpu_custom_call" | custom-call | tf_op jit(solution)/shard_map/scale/pallas_call | solution.py:586

commit v11 on v10

--- a/solution.py
+++ b/solution.py
@@ -125,6 +125,8 @@
 LAST_R = 5
 LAST_C = 4
 SPLIT = 7
+SHIFT_Z = 2
+SHIFT_X = 1
 
 
 def span(first, last):
@@ -193,9 +195,16 @@
     started = []
     waited = set()
 
-    def send(src, dst, part, peer, into=None):
-        k = len(started)
-        copy = pltpu.make_async_remote_copy(
+    def either(part, act):
+        if isinstance(part, tuple):
+            flag, held, plain = part
+            pl.when(flag)(lambda: act(held))
+            pl.when(jnp.logical_not(flag))(lambda: act(plain))
+        else:
+            act(part)
+
+    def copy_of(k, src, dst, part, into, peer):
+        return pltpu.make_async_remote_copy(
             src_ref=src.at[part],
             dst_ref=dst.at[part if into is None else into],
             send_sem=send_sems.at[k],
@@ -203,20 +212,27 @@
             device_id=peer,
             device_id_type=MESH,
         )
-        copy.start()
-        started.append(copy)
+
+    def send(src, dst, part, peer, into=None):
+        k = len(started)
+        either(part, lambda p: copy_of(k, src, dst, p, into, peer).start())
+        started.append((part, lambda p: copy_of(k, src, dst, p, into, peer).wait_send()))
         return k
 
     def arrived(k, dst, part, peer):
         waited.add(k)
-        pltpu.make_async_remote_copy(
-            src_ref=dst.at[part],
-            dst_ref=dst.at[part],
-            send_sem=send_sems.at[k],
-            recv_sem=recv_sems.at[k],
-            device_id=peer,
-            device_id_type=MESH,
-        ).wait_recv()
+        either(part, lambda p: copy_of(k, dst, dst, p, None, peer).wait_recv())
+
+    def halves(place, shift):
+        cut = HALF - shift
+        pairs = []
+        for step in (0, 3, 1, 2):
+            flag = (place + step) % 4 == 2
+            pairs.append(((flag, span(0, cut), H1), (flag, span(cut, MAXNZ), H2)))
+        return pairs
+
+    (A1, A2), (M1, M2), (P1, P2), (F1, F2) = halves(z, SHIFT_Z)
+    (B1, B2), (N1, N2), (Q1, Q2), (G1, G2) = halves(x, SHIFT_X)
 
     def other(q):
         return q + 1 - 2 * (q % 2)
@@ -241,15 +257,15 @@
     ym_c, yp_c, yy_c = (across(along_x(s)) for s in (3, 1, 2))
 
     lo1 = send(share_ref, own_r, U1, lo)
-    zp1 = send(share_ref, own_r, H1, zp)
-    zm2 = send(share_ref, own_r, H2, zm)
-    xp1 = send(share_ref, own_c, H1, xp)
-    xm2 = send(share_ref, own_c, H2, xm)
+    zp1 = send(share_ref, own_r, A1, zp)
+    zm2 = send(share_ref, own_r, A2, zm)
+    xp1 = send(share_ref, own_c, B1, xp)
+    xm2 = send(share_ref, own_c, B2, xm)
     lo2 = send(share_ref, own_r, U2, lo)
-    zp2 = send(share_ref, own_r, H2, zp)
-    zm1 = send(share_ref, own_r, H1, zm)
-    xp2 = send(share_ref, own_c, H2, xp)
-    xm1 = send(share_ref, own_c, H1, xm)
+    zp2 = send(share_ref, own_r, A2, zp)
+    zm1 = send(share_ref, own_r, A1, zm)
+    xp2 = send(share_ref, own_c, B2, xp)
+    xm1 = send(share_ref, own_c, B1, xm)
     lo3 = send(share_ref, own_r, L, lo)
     sb0 = send(share_ref, own_r, ALL, sib)
     for copy in keep:
@@ -259,14 +275,14 @@
     arrived(lo1, y_r, U1, lo)
     hi1 = send(y_r, own_c, U1, hi)
     yzp1 = send(y_r, y_r, U1, zp)
-    arrived(zp1, zm_r, H1, zm)
-    fzp = send(zm_r, zm_r, H1, zp)
-    arrived(zm2, zp_r, H2, zp)
-    fzm = send(zp_r, zp_r, H2, zm)
-    arrived(xp1, xm_c, H1, xm)
-    fxp = send(xm_c, xm_c, H1, xp)
-    arrived(xm2, xp_c, H2, xp)
-    fxm = send(xp_c, xp_c, H2, xm)
+    arrived(zp1, zm_r, M1, zm)
+    fzp = send(zm_r, zm_r, M1, zp)
+    arrived(zm2, zp_r, P2, zp)
+    fzm = send(zp_r, zp_r, P2, zm)
+    arrived(xp1, xm_c, N1, xm)
+    fxp = send(xm_c, xm_c, N1, xp)
+    arrived(xm2, xp_c, Q2, xp)
+    fxm = send(xp_c, xp_c, Q2, xm)
     txp = send(xp_c, relay.at[0], K, lo, T)
     lzp = send(zp_r, zp_r, L, lo)
     arrived(lo2, y_r, U2, lo)
@@ -280,12 +296,12 @@
     hi3 = send(y_r, own_c, L, hi)
     sb1 = send(y_r, y_r, ALL, sib)
 
-    arrived(zp2, zm_r, H2, zm)
-    arrived(xp2, xm_c, H2, xm)
+    arrived(zp2, zm_r, M2, zm)
+    arrived(xp2, xm_c, N2, xm)
     txm = send(xm_c, relay.at[1], K, lo, T)
     lzm = send(zm_r, zm_r, L, lo)
     sb2 = send(zm_r, zm_r, ALL, sib)
-    arrived(zm1, zp_r, H1, zp)
+    arrived(zm1, zp_r, P1, zp)
     sb3 = send(zp_r, zp_r, ALL, sib)
     arrived(hi2, y_c, U2, hi)
     arrived(hi3, y_c, L, hi)
@@ -294,11 +310,11 @@
     yxm1 = send(y_c, y_c, U1, xm)
     arrived(txp, relay.at[0], T, lo)
     uxp = send(relay.at[0], xp_c, T, hi, K)
-    arrived(fxm, xx_c, H2, xp)
+    arrived(fxm, xx_c, G2, xp)
     txx = send(xx_c, relay.at[2], K, lo, T)
-    arrived(fzm, zz_r, H2, zp)
+    arrived(fzm, zz_r, F2, zp)
     lzz = send(zz_r, zz_r, L, lo)
-    arrived(fzp, zz_r, H1, zm)
+    arrived(fzp, zz_r, F1, zm)
     sb4 = send(zz_r, zz_r, ALL, sib)
     arrived(txm, relay.at[1], T, lo)
     uxm = send(relay.at[1], xm_c, T, hi, K)
@@ -330,8 +346,8 @@
     sb7 = send(yy_r, yy_r, L, sib)
     for copy in keep:
         copy.wait()
-    arrived(xm1, xp_c, H1, xp)
-    arrived(fxp, xx_c, H1, xm)
+    arrived(xm1, xp_c, Q1, xp)
+    arrived(fxp, xx_c, G1, xm)
     arrived(yxm1, yp_c, U1, xp)
     arrived(sb0, rsib(col), ALL, sib)
     arrived(sb1, rsib(mate), ALL, sib)
@@ -369,8 +385,8 @@
     arrived(sb10, rsib(other(along_z(2))), V4, sib)
     arrived(sb11, rsib(other(along_z(2))), V2, sib)
     assert waited == set(range(len(started))) and len(started) == COPIES
-    for copy in started:
-        copy.wait_send()
+    for part, wait in started:
+        either(part, wait)
     hand.wait()
 
 

time: 57 us -> 55 us (0.965)
  Pallas kernels: 56.9 us -> 54.9 us
    pallas_call x1, Pallas kernels: 10 us -> 9.07 us  [product(): pl.pallas_call(product_kernel, out_shape=[pltpu.VMEM(shape, jnp.float32),...]
    pallas_call x1, Pallas kernels: 44 us -> 43.2 us  [gather(): pl.pallas_call(gather_kernel, out_shape=[pltpu.VMEM((17, SHARE, BLK), dty...]
where the time goes in v11:
time: 55 us; the launch traced here: 54.9 us
  Pallas kernels  54.9 us (100%)
    pallas_call x1, Pallas kernels, gather(): pl.pallas_call(gather_kernel, out_shape=[pltpu.VMEM((17, SHARE, BLK), dty...  43.2 us
    pallas_call x1, Pallas kernels, product(): pl.pallas_call(product_kernel, out_shape=[pltpu.VMEM(shape, jnp.float32),...  9.07 us
    pallas_call x1, Pallas kernels, scale(): pl.pallas_call(functools.partial(scale_kernel, scaling), out_shape=jax.Sh...  2.29 us

profile of v11, /device:TPU:0, one launch (start us, length us, event | category | flops | bytes accessed | tf_op | source)
XLA Modules:
  0.0 54.9 jit_solution(9671683915354805058)
XLA Ops:
  0.0 43.2 %gather.1 = (bf16[17,2432,128]{2,1,0:T(8,128)(2,1)S(1)}, bf16[8,2432,128]{2,1,0:T(8,128)(2,1)S(1)}, s32[16,128]{1,0:T(8,128)S(4)}) custom-call(s32[6,12]{1,0:T(8,128)} %bitcast.1, bf16[1536,768]{1,0:T(8,128)(2,1)} %x_ref.1), custom_call_target="tpu_custom_call" | custom-call | tf_op jit(solution)/shard_map/gather/pallas_call | solution.py:399
  43.3 0.2 later.1.extra_ref
  43.5 9.1 %product.1 = (f32[1536,768]{1,0:T(8,128)S(1)}, f32[1,768]{1,0:T(1,128)S(1)}) custom-call(bf16[17,2432,128]{2,1,0:T(8,128)(2,1)S(1)} %get-tuple-element.10.rows_ref, bf16[8,2432,128]{2,1,0:T(8,128)(2,1)S(1)} %get-tuple-element.11.cols_ref, s32[16,128]{1,0:T(8,128)S(4)} %get-tuple-element.12.table_ref, f32[73,128,128]{2,1,0:T(8,128)S(1)} %later.1.extra_ref), custom_call_target="tpu_custom_call" | custom-call | tf_op jit(solution)/shard_map/product/pallas_call | solution.py:566
  52.6 2.3 %scale.1 = f32[1536,768]{1,0:T(8,128)} custom-call(f32[1536,768]{1,0:T(8,128)S(1)} %get-tuple-element.13.value_ref, f32[1,768]{1,0:T(1,128)S(1)} %get-tuple-element.14.total_ref), custom_call_target="tpu_custom_call" | custom-call | tf_op jit(solution)/shard_map/scale/pallas_call | solution.py:602

commit v12 on v11

--- a/solution.py
+++ b/solution.py
@@ -515,7 +515,9 @@
     rows_ref, cols_ref, table_ref, extra_ref, out_ref, total_ref, slots, send_sems, recv_sems
 ):
     row, col, layer = (lax.axis_index(a) for a in ("row", "col", "layer"))
-    peers = [((row + s) % 8, col, layer) for s in range(1, 8)]
+    high, x = row // 4, row % 4
+    steps = [(1, 2), (1, 1), (1, 3), (1, 0), (0, 2), (0, 1), (0, 3)]
+    peers = [((high + h) % 2 * 4 + (x + d) % 4, col, layer) for h, d in steps]
     barrier = pltpu.get_barrier_semaphore()
     for peer in peers:
         pl.semaphore_signal(barrier, inc=1, device_id=peer, device_id_type=MESH)

time: 55 us -> 55.4 us (level)
  no operation moved by 1% of the time
where the time goes in v12:
time: 55.4 us; the launch traced here: 54.8 us
  Pallas kernels  54.8 us (99%)
    pallas_call x1, Pallas kernels, gather(): pl.pallas_call(gather_kernel, out_shape=[pltpu.VMEM((17, SHARE, BLK), dty...  43.2 us
    pallas_call x1, Pallas kernels, product(): pl.pallas_call(product_kernel, out_shape=[pltpu.VMEM(shape, jnp.float32),...  8.74 us
    pallas_call x1, Pallas kernels, scale(): pl.pallas_call(functools.partial(scale_kernel, scaling), out_shape=jax.Sh...  2.29 us

profile of v12, /device:TPU:0, one launch (start us, length us, event | category | flops | bytes accessed | tf_op | source)
XLA Modules:
  0.0 54.8 jit_solution(8020004612437244224)
XLA Ops:
  0.0 43.2 %gather.1 = (bf16[17,2432,128]{2,1,0:T(8,128)(2,1)S(1)}, bf16[8,2432,128]{2,1,0:T(8,128)(2,1)S(1)}, s32[16,128]{1,0:T(8,128)S(4)}) custom-call(s32[6,12]{1,0:T(8,128)} %bitcast.1, bf16[1536,768]{1,0:T(8,128)(2,1)} %x_ref.1), custom_call_target="tpu_custom_call" | custom-call | tf_op jit(solution)/shard_map/gather/pallas_call | solution.py:399
  43.3 0.6 %later.1.extra_ref = f32[73,128,128]{2,1,0:T(8,128)S(1)} custom-call(bf16[17,2432,128]{2,1,0:T(8,128)(2,1)S(1)} %get-tuple-element.10.rows_ref, bf16[8,2432,128]{2,1,0:T(8,128)(2,1)S(1)} %get-tuple-element.11.cols_ref, s32[16,128]{1,0:T(8,128)S(4)} %get-tuple-element.12.table_ref), custom_call_target="tpu_custom_call" | custom-call | tf_op jit(solution)/shard_map/later/pallas_call | solution.py:498
  43.8 8.7 %product.1 = (f32[1536,768]{1,0:T(8,128)S(1)}, f32[1,768]{1,0:T(1,128)S(1)}) custom-call(bf16[17,2432,128]{2,1,0:T(8,128)(2,1)S(1)} %get-tuple-element.10.rows_ref, bf16[8,2432,128]{2,1,0:T(8,128)(2,1)S(1)} %get-tuple-element.11.cols_ref, s32[16,128]{1,0:T(8,128)S(4)} %get-tuple-element.12.table_ref, f32[73,128,128]{2,1,0:T(8,128)S(1)} %later.1.extra_ref), custom_call_target="tpu_custom_call" | custom-call | tf_op jit(solution)/shard_map/product/pallas_call | solution.py:568
  52.6 2.3 %scale.1 = f32[1536,768]{1,0:T(8,128)} custom-call(f32[1536,768]{1,0:T(8,128)S(1)} %get-tuple-element.13.value_ref, f32[1,768]{1,0:T(1,128)S(1)} %get-tuple-element.14.total_ref), custom_call_target="tpu_custom_call" | custom-call | tf_op jit(solution)/shard_map/scale/pallas_call | solution.py:604

commit v13 on v12

--- a/solution.py
+++ b/solution.py
@@ -10,7 +10,8 @@
 BLK = 128
 MAXNZ = 18
 HEAD = 32
-HALF = MAXNZ // 2
+HALF_Z = 8
+HALF_X = 9
 SLOTS = MAXNZ + 1
 SHARE = SLOTS * BLK
 TOP = BLK - HEAD
@@ -123,15 +124,15 @@
 
 
 LAST_R = 5
-LAST_C = 4
-SPLIT = 7
+LAST_C = 4.5
+SPLIT = 6.5
 SHIFT_Z = 2
 SHIFT_X = 1
 
 
 def span(first, last):
-    low = (first + 1) * BLK if first else TOP
-    return pl.ds(low, (last + 1) * BLK - low)
+    low = int((first + 1) * BLK) if first else TOP
+    return pl.ds(low, int((last + 1) * BLK) - low)
 
 
 def gather_kernel(
@@ -187,11 +188,10 @@
     ]
 
     EARLY, EARLY_C = MAXNZ - LAST_R, MAXNZ - LAST_C
-    H1, H2 = span(0, HALF), span(HALF, MAXNZ)
     U1, U2, L = span(0, SPLIT), span(SPLIT, EARLY), span(EARLY, MAXNZ)
     V1, V2, V3, V4 = span(0, 4), span(4, SPLIT), span(SPLIT, 10), span(10, EARLY)
     W2, K = span(SPLIT, EARLY_C), span(EARLY_C, MAXNZ)
-    T = pl.ds(0, LAST_C * BLK)
+    T = pl.ds(0, int(LAST_C * BLK))
     started = []
     waited = set()
 
@@ -223,16 +223,17 @@
         waited.add(k)
         either(part, lambda p: copy_of(k, dst, dst, p, None, peer).wait_recv())
 
-    def halves(place, shift):
-        cut = HALF - shift
+    def halves(place, half, shift):
+        cut = half - shift
         pairs = []
         for step in (0, 3, 1, 2):
             flag = (place + step) % 4 == 2
-            pairs.append(((flag, span(0, cut), H1), (flag, span(cut, MAXNZ), H2)))
+            first = (flag, span(0, cut), span(0, half))
+            pairs.append((first, (flag, span(cut, MAXNZ), span(half, MAXNZ))))
         return pairs
 
-    (A1, A2), (M1, M2), (P1, P2), (F1, F2) = halves(z, SHIFT_Z)
-    (B1, B2), (N1, N2), (Q1, Q2), (G1, G2) = halves(x, SHIFT_X)
+    (A1, A2), (M1, M2), (P1, P2), (F1, F2) = halves(z, HALF_Z, SHIFT_Z)
+    (B1, B2), (N1, N2), (Q1, Q2), (G1, G2) = halves(x, HALF_X, SHIFT_X)
 
     def other(q):
         return q + 1 - 2 * (q % 2)
@@ -413,7 +414,7 @@
             pltpu.SMEM(block_mask.shape[::-1], jnp.int32),
             pltpu.VMEM((cells, BLK, BLK), dtype),
             pltpu.VMEM((SHARE, BLK), dtype),
-            pltpu.VMEM((3, LAST_C * BLK, BLK), dtype),
+            pltpu.VMEM((3, int(LAST_C * BLK), BLK), dtype),
             pltpu.VMEM((8, BLK), jnp.int32),
             pltpu.SMEM((8, BLK), jnp.int32),
             pltpu.SemaphoreType.DMA((COPIES,)),

time: 55.4 us -> 55.9 us (level)
  Pallas kernels: 54.8 us -> 55.6 us
    pallas_call x1, Pallas kernels: 8.74 us -> 9.68 us  [product(): pl.pallas_call(product_kernel, out_shape=[pltpu.VMEM(shape, jnp.float32),...]
where the time goes in v13:
time: 55.9 us; the launch traced here: 55.7 us
  Pallas kernels  55.6 us (99%)
    pallas_call x1, Pallas kernels, gather(): pl.pallas_call(gather_kernel, out_shape=[pltpu.VMEM((17, SHARE, BLK), dty...  43.1 us
    pallas_call x1, Pallas kernels, product(): pl.pallas_call(product_kernel, out_shape=[pltpu.VMEM(shape, jnp.float32),...  9.68 us
    pallas_call x1, Pallas kernels, scale(): pl.pallas_call(functools.partial(scale_kernel, scaling), out_shape=jax.Sh...  2.29 us

profile of v13, /device:TPU:0, one launch (start us, length us, event | category | flops | bytes accessed | tf_op | source)
XLA Modules:
  0.0 55.7 jit_solution(10822608706169070341)
XLA Ops:
  0.0 43.1 %gather.1 = (bf16[17,2432,128]{2,1,0:T(8,128)(2,1)S(1)}, bf16[8,2432,128]{2,1,0:T(8,128)(2,1)S(1)}, s32[16,128]{1,0:T(8,128)S(4)}) custom-call(s32[6,12]{1,0:T(8,128)} %bitcast.1, bf16[1536,768]{1,0:T(8,128)(2,1)} %x_ref.1), custom_call_target="tpu_custom_call" | custom-call | tf_op jit(solution)/shard_map/gather/pallas_call | solution.py:400
  43.1 0.5 later.1.extra_ref
  43.7 9.7 %product.1 = (f32[1536,768]{1,0:T(8,128)S(1)}, f32[1,768]{1,0:T(1,128)S(1)}) custom-call(bf16[17,2432,128]{2,1,0:T(8,128)(2,1)S(1)} %get-tuple-element.10.rows_ref, bf16[8,2432,128]{2,1,0:T(8,128)(2,1)S(1)} %get-tuple-element.11.cols_ref, s32[16,128]{1,0:T(8,128)S(4)} %get-tuple-element.12.table_ref, f32[73,128,128]{2,1,0:T(8,128)S(1)} %later.1.extra_ref), custom_call_target="tpu_custom_call" | custom-call | tf_op jit(solution)/shard_map/product/pallas_call | solution.py:569
  53.4 2.3 %scale.1 = f32[1536,768]{1,0:T(8,128)} custom-call(f32[1536,768]{1,0:T(8,128)S(1)} %get-tuple-element.13.value_ref, f32[1,768]{1,0:T(1,128)S(1)} %get-tuple-element.14.total_ref), custom_call_target="tpu_custom_call" | custom-call | tf_op jit(solution)/shard_map/scale/pallas_call | solution.py:605

commit v14 on v12

--- a/solution.py
+++ b/solution.py
@@ -445,7 +445,7 @@
     return ref.reshape(ref.shape[0] * SLOTS, BLK, BLK)
 
 
-AT_ONCE = 4
+AT_ONCE = 8
 
 
 def later_kernel(rows_ref, cols_ref, table_ref, extra_ref, table_v, table_s, list_s, sem):

time: 55.4 us -> 55.7 us (level)
  no operation moved by 1% of the time
where the time goes in v14:
time: 55.7 us; the launch traced here: 55 us
  Pallas kernels  55 us (99%)
    pallas_call x1, Pallas kernels, gather(): pl.pallas_call(gather_kernel, out_shape=[pltpu.VMEM((17, SHARE, BLK), dty...  43.2 us
    pallas_call x1, Pallas kernels, product(): pl.pallas_call(product_kernel, out_shape=[pltpu.VMEM(shape, jnp.float32),...  8.76 us
    pallas_call x1, Pallas kernels, scale(): pl.pallas_call(functools.partial(scale_kernel, scaling), out_shape=jax.Sh...  2.29 us

profile of v14, /device:TPU:0, one launch (start us, length us, event | category | flops | bytes accessed | tf_op | source)
XLA Modules:
  0.0 55.0 jit_solution(6318004322382564271)
XLA Ops:
  0.0 43.2 %gather.1 = (bf16[17,2432,128]{2,1,0:T(8,128)(2,1)S(1)}, bf16[8,2432,128]{2,1,0:T(8,128)(2,1)S(1)}, s32[16,128]{1,0:T(8,128)S(4)}) custom-call(s32[6,12]{1,0:T(8,128)} %bitcast.1, bf16[1536,768]{1,0:T(8,128)(2,1)} %x_ref.1), custom_call_target="tpu_custom_call" | custom-call | tf_op jit(solution)/shard_map/gather/pallas_call | solution.py:399
  43.3 0.7 %later.1.extra_ref = f32[73,128,128]{2,1,0:T(8,128)S(1)} custom-call(bf16[17,2432,128]{2,1,0:T(8,128)(2,1)S(1)} %get-tuple-element.10.rows_ref, bf16[8,2432,128]{2,1,0:T(8,128)(2,1)S(1)} %get-tuple-element.11.cols_ref, s32[16,128]{1,0:T(8,128)S(4)} %get-tuple-element.12.table_ref), custom_call_target="tpu_custom_call" | custom-call | tf_op jit(solution)/shard_map/later/pallas_call | solution.py:498
  43.9 8.8 %product.1 = (f32[1536,768]{1,0:T(8,128)S(1)}, f32[1,768]{1,0:T(1,128)S(1)}) custom-call(bf16[17,2432,128]{2,1,0:T(8,128)(2,1)S(1)} %get-tuple-element.10.rows_ref, bf16[8,2432,128]{2,1,0:T(8,128)(2,1)S(1)} %get-tuple-element.11.cols_ref, s32[16,128]{1,0:T(8,128)S(4)} %get-tuple-element.12.table_ref, f32[73,128,128]{2,1,0:T(8,128)S(1)} %later.1.extra_ref), custom_call_target="tpu_custom_call" | custom-call | tf_op jit(solution)/shard_map/product/pallas_call | solution.py:568
  52.7 2.3 %scale.1 = f32[1536,768]{1,0:T(8,128)} custom-call(f32[1536,768]{1,0:T(8,128)S(1)} %get-tuple-element.13.value_ref, f32[1,768]{1,0:T(1,128)S(1)} %get-tuple-element.14.total_ref), custom_call_target="tpu_custom_call" | custom-call | tf_op jit(solution)/shard_map/scale/pallas_call | solution.py:604

commit v15 on v14

--- a/solution.py
+++ b/solution.py
@@ -539,7 +539,7 @@
         return tuple(out)
 
     sums = tuple(jnp.zeros((8, BLK), jnp.float32) for _ in range(wide))
-    sums = lax.fori_loop(0, tiles, one_row, sums, unroll=6)
+    sums = lax.fori_loop(0, tiles, one_row, sums, unroll=12)
     slots[row] = jnp.concatenate([jnp.sum(v, axis=0, keepdims=True) for v in sums], 1)
     pl.semaphore_wait(barrier, 7)
     copies = [

time: 55.7 us -> 55 us (0.987)
  no operation moved by 1% of the time
where the time goes in v15:
time: 55 us; the launch traced here: 54.6 us
  Pallas kernels  54.6 us (99%)
    pallas_call x1, Pallas kernels, gather(): pl.pallas_call(gather_kernel, out_shape=[pltpu.VMEM((17, SHARE, BLK), dty...  43.2 us
    pallas_call x1, Pallas kernels, product(): pl.pallas_call(product_kernel, out_shape=[pltpu.VMEM(shape, jnp.float32),...  8.39 us
    pallas_call x1, Pallas kernels, scale(): pl.pallas_call(functools.partial(scale_kernel, scaling), out_shape=jax.Sh...  2.29 us

profile of v15, /device:TPU:0, one launch (start us, length us, event | category | flops | bytes accessed | tf_op | source)
XLA Modules:
  0.0 54.6 jit_solution(248765334592653298)
XLA Ops:
  0.0 43.2 %gather.1 = (bf16[17,2432,128]{2,1,0:T(8,128)(2,1)S(1)}, bf16[8,2432,128]{2,1,0:T(8,128)(2,1)S(1)}, s32[16,128]{1,0:T(8,128)S(4)}) custom-call(s32[6,12]{1,0:T(8,128)} %bitcast.1, bf16[1536,768]{1,0:T(8,128)(2,1)} %x_ref.1), custom_call_target="tpu_custom_call" | custom-call | tf_op jit(solution)/shard_map/gather/pallas_call | solution.py:399
  43.3 0.7 %later.1.extra_ref = f32[73,128,128]{2,1,0:T(8,128)S(1)} custom-call(bf16[17,2432,128]{2,1,0:T(8,128)(2,1)S(1)} %get-tuple-element.10.rows_ref, bf16[8,2432,128]{2,1,0:T(8,128)(2,1)S(1)} %get-tuple-element.11.cols_ref, s32[16,128]{1,0:T(8,128)S(4)} %get-tuple-element.12.table_ref), custom_call_target="tpu_custom_call" | custom-call | tf_op jit(solution)/shard_map/later/pallas_call | solution.py:498
  43.9 8.4 %product.1 = (f32[1536,768]{1,0:T(8,128)S(1)}, f32[1,768]{1,0:T(1,128)S(1)}) custom-call(bf16[17,2432,128]{2,1,0:T(8,128)(2,1)S(1)} %get-tuple-element.10.rows_ref, bf16[8,2432,128]{2,1,0:T(8,128)(2,1)S(1)} %get-tuple-element.11.cols_ref, s32[16,128]{1,0:T(8,128)S(4)} %get-tuple-element.12.table_ref, f32[73,128,128]{2,1,0:T(8,128)S(1)} %later.1.extra_ref), custom_call_target="tpu_custom_call" | custom-call | tf_op jit(solution)/shard_map/product/pallas_call | solution.py:568
  52.3 2.3 %scale.1 = f32[1536,768]{1,0:T(8,128)} custom-call(f32[1536,768]{1,0:T(8,128)S(1)} %get-tuple-element.13.value_ref, f32[1,768]{1,0:T(1,128)S(1)} %get-tuple-element.14.total_ref), custom_call_target="tpu_custom_call" | custom-call | tf_op jit(solution)/shard_map/scale/pallas_call | solution.py:604
